TPU v7x, 128 devices: a whole 4x4x4 slice. The times are simulated.
128 devices in a mesh: row: 32 (over x, z_lo, y), col: 4 (over z_hi, core).
Axes of the slice: x: 4, y: 4, z: 4 (z_hi: 2, z_lo: 2; z = z_hi * 2 + z_lo), core: 2. Of those that a mesh axis runs over, the one named last changes fastest.
Arguments:
- query_near: bfloat16 [128, 512, 256], P('row', 'col'), may hold values from -9 to 9
- key_near: bfloat16 [128, 512, 256], P('row', 'col'), may hold values from -9 to 9
- value_near: bfloat16 [128, 512, 256], P('row', 'col'), may hold values from -6 to 6
- dilated_queries: bfloat16 [128, 512, 256], P('row', 'col'), may hold values from -9 to 9
- dilated_keys: bfloat16 [128, 512, 256], P('row', 'col'), may hold values from -9 to 9
- dilated_values: bfloat16 [128, 512, 256], P('row', 'col'), may hold values from -6 to 6
Outputs:
- attended_near: bfloat16 [128, 512, 256], P('row', 'col')
- dilated_attention_output: bfloat16 [128, 512, 256], P('row', 'col')
All inputs are finite; a program needn't handle non-finite values.
Results may differ from a plain program's by a relative error of at most 0.0049.
Values may be sent and summed in bfloat16 or wider, within the bound.
A program may use at most 192 MiB of HBM per device.

v0:
```python
import math

import jax
import jax.numpy as jnp
from jax import lax
from jax.sharding import PartitionSpec as P

HEADS = 4
DILATION_STEP = 16


def passed_along(block, axis, distance):
    devices = range(lax.axis_size(axis))
    route = [(i - distance, i) for i in devices if i - distance in devices]
    return lax.ppermute(block, axis, route)


def with_halo(cells, sides, width):
    for axis, dim in sides:
        count = lax.axis_size(axis)
        ends = count - 1
        head = lax.slice_in_dim(cells, 0, width, axis=dim)
        tail = lax.slice_in_dim(cells, cells.shape[dim] - width, cells.shape[dim], axis=dim)
        cells = jnp.concatenate(
            [
                lax.ppermute(tail, axis, [(i, (i + 1) % count) for i in range(ends)]),
                cells,
                lax.ppermute(head, axis, [((i + 1) % count, i) for i in range(ends)]),
            ],
            axis=dim,
        )
    return cells


def window_attend(
    query, padded, row_spacing, col_spacing, row_places, row_limit, column_begin, complete_width
):
    row_count, col_count, channels = query.shape
    token_count = row_count * col_count
    padded_rows = padded.shape[1]
    head_size = channels // HEADS
    row_margin = 3 * row_spacing
    col_margin = 3 * col_spacing
    scaling = 1.0 / math.sqrt(head_size)
    channel_heads = jnp.arange(channels, dtype=jnp.int32) // head_size
    head_table = channel_heads[None, :] == jnp.arange(HEADS, dtype=jnp.int32)[:, None]
    table_wide = head_table.astype(jnp.float32)
    table_narrow = head_table.astype(jnp.bfloat16)
    query_flat = query.reshape(token_count, channels).astype(jnp.float32)
    col_ids = column_begin + jnp.arange(col_count, dtype=jnp.int32)
    row_flat = jnp.repeat(row_places, col_count)
    col_flat = jnp.tile(col_ids, row_count)
    head_sum = (((1,), (1,)), ((), ()))
    head_spread = (((0,), (0,)), ((), ()))

    def column_view(tap_col, which):
        second = col_margin + tap_col * col_spacing
        return padded[which, :, second : second + col_count].reshape(
            padded_rows * col_count, channels
        )

    score_list = []
    for tap_col in range(-3, 4):
        key_view = column_view(tap_col, 0)
        moved_col = col_flat + tap_col * col_spacing
        inside_col = (moved_col >= 0) & (moved_col < complete_width)
        for tap_row in range(-3, 4):
            first = (row_margin + tap_row * row_spacing) * col_count
            key_tile = key_view[first : first + token_count]
            product = query_flat * key_tile.astype(jnp.float32)
            scores = (
                lax.dot_general(
                    table_wide,
                    product,
                    head_sum,
                    precision=lax.Precision.HIGHEST,
                    preferred_element_type=jnp.float32,
                )
                * scaling
            )
            moved_row = row_flat + tap_row * row_spacing
            inside = inside_col & (moved_row >= 0) & (moved_row < row_limit)
            score_list.append(jnp.where(inside[None, :], scores, -jnp.inf))
    scores = jnp.stack(score_list)
    peak = jnp.max(scores, axis=0)
    weights = jnp.exp(scores - peak[None])
    total = jnp.sum(weights, axis=0)
    probs = (weights / total[None]).astype(jnp.bfloat16)
    accum = jnp.zeros((token_count, channels), jnp.float32)
    position = 0
    for tap_col in range(-3, 4):
        value_view = column_view(tap_col, 1)
        for tap_row in range(-3, 4):
            first = (row_margin + tap_row * row_spacing) * col_count
            value_tile = value_view[first : first + token_count]
            spread = lax.dot_general(
                probs[position], table_narrow, head_spread, preferred_element_type=jnp.float32
            )
            accum = accum + spread * value_tile.astype(jnp.float32)
            position = position + 1
    return accum.reshape(row_count, col_count, channels).astype(jnp.bfloat16)


def fetch_rows(source, distance):
    return passed_along(source, "row", distance)


def extend_rows(source, shard_count):
    rows_above = [fetch_rows(source, distance) for distance in range(shard_count, 0, -1)]
    rows_below = [fetch_rows(source, -distance) for distance in range(1, shard_count + 1)]
    return jnp.concatenate(rows_above + [source] + rows_below, axis=1)


def per_device(query_near, key_near, value_near, dilated_queries, dilated_keys, dilated_values):
    row_count, col_count, channels = query_near.shape
    device_count = lax.axis_size("row")
    image_height = row_count * device_count
    complete_width = col_count * lax.axis_size("col")
    place = lax.axis_index("row")
    row_start = place * row_count
    column_begin = lax.axis_index("col") * col_count
    local_rows = row_start + jnp.arange(row_count, dtype=jnp.int32)
    near_pad = with_halo(jnp.stack((key_near, value_near)), (("row", 1), ("col", 2)), 3)
    attended_near = window_attend(
        query_near, near_pad, 1, 1, local_rows, image_height, column_begin, complete_width
    )
    extent_rows = 3 * DILATION_STEP
    shard_count = extent_rows // row_count
    far_pair = jnp.stack((dilated_keys, dilated_values))
    tall_pad = extend_rows(far_pair, shard_count)
    dilated_padding = with_halo(tall_pad, (("col", 2),), extent_rows)
    dilated_attention_output = window_attend(
        dilated_queries,
        dilated_padding,
        DILATION_STEP,
        DILATION_STEP,
        local_rows,
        image_height,
        column_begin,
        complete_width,
    )
    return (attended_near, dilated_attention_output)


def solution(mesh):
    placed = (
        P("row", "col", None),
        P("row", "col", None),
        P("row", "col", None),
        P("row", "col", None),
        P("row", "col", None),
        P("row", "col", None),
    )
    return jax.shard_map(
        per_device,
        mesh=mesh,
        in_specs=placed,
        out_specs=(P("row", "col", None), P("row", "col", None)),
        check_vma=False,
    )
```

profile of v0, /device:TPU:43, one launch (start us, length us, event | category | flops | bytes accessed | tf_op | source)
XLA Modules:
  0.0 537.6 jit_solution(4381130449778839138)
XLA Ops:
  1.8 3.3 collective-permute-start.4
  5.1 1.9 collective-permute-start.5
  7.0 2.2 collective-permute-start.6
  9.2 2.2 fusion.294
  11.4 2.9 collective-permute-start
  14.3 2.4 collective-permute-start.1
  18.8 4.5 collective-permute-done
  23.3 2.5 collective-permute-done.1
  26.6 6.9 %collective-permute-start.2 = (bf16[2,10,3,256]{3,2,1,0:T(4,128)(2,1)S(1)}, bf16[2,10,3,256]{3,2,1,0:T(4,128)(2,1)S(1)}, u32[]{:S(2)}, u32[]{:S(2)}) collective-permute-start(bf16[2,10,3,256]{3,2,1,0:T(4,128)(2,1)S(1)} %get-tuple-element.175), channel_id=1, source_target_pairs={{0,1},{1,2},{2,3},{4,5},{5,6},{6,7},{8,9},{9,10},{10,11},{12,13},{... | collective-permute-start | bytes 92168 | tf_op jit(solution)/shard_map/ppermute | solution.py:26
  33.6 1.9 collective-permute-start.3
  38.3 23.1 %collective-permute-start.7 = (bf16[2,4,128,256]{3,2,1,0:T(8,128)(2,1)S(1)}, bf16[2,4,128,256]{3,2,1,0:T(8,128)(2,1)S(1)}, u32[]{:S(2)}, u32[]{:S(2)}) collective-permute-start(bf16[2,4,128,256]{3,2,1,0:T(8,128)(2,1)S(1)} %pad_maximum_fusion.2), channel_id=1, source_target_pairs={{0,36},{4,40},{8,44},{12,48},{16,52},{20,56},{24,60},{28,64},{32,6... | collective-permute-start | bytes 1572872 | tf_op jit(solution)/shard_map/ppermute | solution.py:15
  61.4 3.3 collective-permute-start.8
  136.0 2.7 collective-permute-start.9
  139.5 4.7 collective-permute-start.10
  145.1 1.9 collective-permute-start.11
  150.7 3.0 collective-permute-start.13
  154.6 4.8 collective-permute-start.14
  160.2 8.5 %collective-permute-done.10 = bf16[2,4,128,256]{3,2,1,0:T(8,128)(2,1)S(1)} collective-permute-done((bf16[2,4,128,256]{3,2,1,0:T(8,128)(2,1)S(1)}, bf16[2,4,128,256]{3,2,1,0:T(8,128)(2,1)S(1)}, u32[]{:S(2)}, u32[]{:S(2)}) %collective-permute-start.10) | collective-permute-done | bytes 524320 | tf_op jit(solution)/shard_map/ppermute | solution.py:15
  168.7 8.6 %collective-permute-start.15 = (bf16[2,4,128,256]{3,2,1,0:T(8,128)(2,1)S(1)}, bf16[2,4,128,256]{3,2,1,0:T(8,128)(2,1)S(1)}, u32[]{:S(2)}, u32[]{:S(2)}) collective-permute-start(bf16[2,4,128,256]{3,2,1,0:T(8,128)(2,1)S(1)} %pad_maximum_fusion.2), channel_id=1, source_target_pairs={{0,4},{4,8},{8,12},{12,16},{16,20},{20,24},{24,28},{28,32},{32,36}... | collective-permute-start | bytes 1572872 | tf_op jit(solution)/shard_map/ppermute | solution.py:15
  178.2 4.9 collective-permute-start.16
  183.9 10.6 %collective-permute-done.12 = bf16[2,4,128,256]{3,2,1,0:T(8,128)(2,1)S(1)} collective-permute-done((bf16[2,4,128,256]{3,2,1,0:T(8,128)(2,1)S(1)}, bf16[2,4,128,256]{3,2,1,0:T(8,128)(2,1)S(1)}, u32[]{:S(2)}, u32[]{:S(2)}) %collective-permute-start.12) | collective-permute-done | bytes 524320 | tf_op jit(solution)/shard_map/ppermute | solution.py:15
  197.8 14.1 %collective-permute-start.18 = (bf16[2,4,128,256]{3,2,1,0:T(8,128)(2,1)S(1)}, bf16[2,4,128,256]{3,2,1,0:T(8,128)(2,1)S(1)}, u32[]{:S(2)}, u32[]{:S(2)}) collective-permute-start(bf16[2,4,128,256]{3,2,1,0:T(8,128)(2,1)S(1)} %pad_maximum_fusion.2), channel_id=1, source_target_pairs={{12,0},{16,4},{20,8},{24,12},{28,16},{32,20},{36,24},{40,28},{44,3... | collective-permute-start | bytes 1572872 | tf_op jit(solution)/shard_map/ppermute | solution.py:15
  212.7 9.2 %collective-permute-start.19 = (bf16[2,4,128,256]{3,2,1,0:T(8,128)(2,1)S(1)}, bf16[2,4,128,256]{3,2,1,0:T(8,128)(2,1)S(1)}, u32[]{:S(2)}, u32[]{:S(2)}) collective-permute-start(bf16[2,4,128,256]{3,2,1,0:T(8,128)(2,1)S(1)} %pad_maximum_fusion.2), channel_id=1, source_target_pairs={{16,0},{20,4},{24,8},{28,12},{32,16},{36,20},{40,24},{44,28},{48,3... | collective-permute-start | bytes 1572872 | tf_op jit(solution)/shard_map/ppermute | solution.py:15
  222.7 8.9 %collective-permute-start.20 = (bf16[2,4,128,256]{3,2,1,0:T(8,128)(2,1)S(1)}, bf16[2,4,128,256]{3,2,1,0:T(8,128)(2,1)S(1)}, u32[]{:S(2)}, u32[]{:S(2)}) collective-permute-start(bf16[2,4,128,256]{3,2,1,0:T(8,128)(2,1)S(1)} %pad_maximum_fusion.2), channel_id=1, source_target_pairs={{20,0},{24,4},{28,8},{32,12},{36,16},{40,20},{44,24},{48,28},{52,3... | collective-permute-start | bytes 1572872 | tf_op jit(solution)/shard_map/ppermute | solution.py:15
  236.1 6.0 %collective-permute-start.22 = (bf16[2,4,128,256]{3,2,1,0:T(8,128)(2,1)S(1)}, bf16[2,4,128,256]{3,2,1,0:T(8,128)(2,1)S(1)}, u32[]{:S(2)}, u32[]{:S(2)}) collective-permute-start(bf16[2,4,128,256]{3,2,1,0:T(8,128)(2,1)S(1)} %pad_maximum_fusion.2), channel_id=1, source_target_pairs={{28,0},{32,4},{36,8},{40,12},{44,16},{48,20},{52,24},{56,28},{60,3... | collective-permute-start | bytes 1572872 | tf_op jit(solution)/shard_map/ppermute | solution.py:15
  242.9 8.8 %collective-permute-start.23 = (bf16[2,4,128,256]{3,2,1,0:T(8,128)(2,1)S(1)}, bf16[2,4,128,256]{3,2,1,0:T(8,128)(2,1)S(1)}, u32[]{:S(2)}, u32[]{:S(2)}) collective-permute-start(bf16[2,4,128,256]{3,2,1,0:T(8,128)(2,1)S(1)} %pad_maximum_fusion.2), channel_id=1, source_target_pairs={{32,0},{36,4},{40,8},{44,12},{48,16},{52,20},{56,24},{60,28},{64,3... | collective-permute-start | bytes 1572872 | tf_op jit(solution)/shard_map/ppermute | solution.py:15
  252.5 7.9 %collective-permute-done.19 = bf16[2,4,128,256]{3,2,1,0:T(8,128)(2,1)S(1)} collective-permute-done((bf16[2,4,128,256]{3,2,1,0:T(8,128)(2,1)S(1)}, bf16[2,4,128,256]{3,2,1,0:T(8,128)(2,1)S(1)}, u32[]{:S(2)}, u32[]{:S(2)}) %collective-permute-start.19) | collective-permute-done | bytes 524320 | tf_op jit(solution)/shard_map/ppermute | solution.py:15
  263.1 20.2 %collective-permute-start.25 = (bf16[2,4,128,256]{3,2,1,0:T(8,128)(2,1)S(1)}, bf16[2,4,128,256]{3,2,1,0:T(8,128)(2,1)S(1)}, u32[]{:S(2)}, u32[]{:S(2)}) collective-permute-start(bf16[2,4,128,256]{3,2,1,0:T(8,128)(2,1)S(1)} %pad_maximum_fusion.2), channel_id=1, source_target_pairs={{40,0},{44,4},{48,8},{52,12},{56,16},{60,20},{64,24},{68,28},{72,3... | collective-permute-start | bytes 1572872 | tf_op jit(solution)/shard_map/ppermute | solution.py:15
  284.2 19.7 %collective-permute-start.26 = (bf16[2,4,128,256]{3,2,1,0:T(8,128)(2,1)S(1)}, bf16[2,4,128,256]{3,2,1,0:T(8,128)(2,1)S(1)}, u32[]{:S(2)}, u32[]{:S(2)}) collective-permute-start(bf16[2,4,128,256]{3,2,1,0:T(8,128)(2,1)S(1)} %pad_maximum_fusion.2), channel_id=1, source_target_pairs={{44,0},{48,4},{52,8},{56,12},{60,16},{64,20},{68,24},{72,28},{76,3... | collective-permute-start | bytes 1572872 | tf_op jit(solution)/shard_map/ppermute | solution.py:15
  304.7 10.2 %collective-permute-start.27 = (bf16[2,4,128,256]{3,2,1,0:T(8,128)(2,1)S(1)}, bf16[2,4,128,256]{3,2,1,0:T(8,128)(2,1)S(1)}, u32[]{:S(2)}, u32[]{:S(2)}) collective-permute-start(bf16[2,4,128,256]{3,2,1,0:T(8,128)(2,1)S(1)} %pad_maximum_fusion.2), channel_id=1, source_target_pairs={{48,0},{52,4},{56,8},{60,12},{64,16},{68,20},{72,24},{76,28},{80,3... | collective-permute-start | bytes 1572872 | tf_op jit(solution)/shard_map/ppermute | solution.py:15
  318.3 4.1 collective-permute-done.26
  323.2 29.5 %collective-permute-done.27 = bf16[2,4,128,256]{3,2,1,0:T(8,128)(2,1)S(1)} collective-permute-done((bf16[2,4,128,256]{3,2,1,0:T(8,128)(2,1)S(1)}, bf16[2,4,128,256]{3,2,1,0:T(8,128)(2,1)S(1)}, u32[]{:S(2)}, u32[]{:S(2)}) %collective-permute-start.27) | collective-permute-done | bytes 524320 | tf_op jit(solution)/shard_map/ppermute | solution.py:15
  354.4 7.0 %fusion.627 = (bf16[2,100,48,256]{3,2,1,0:T(8,128)(2,1)}, bf16[2,100,48,256]{3,2,1,0:T(8,128)(2,1)S(1)}) fusion(bf16[2,100,128,256]{3,2,1,0:T(8,128)(2,1)} %constant_dynamic-update-slice_fusion.49), kind=kLoop, calls=%fused_computation.1361 | loop fusion | bytes 19660800 | tf_op jit(solution)/shard_map/slice | solution.py:22
  361.5 16.1 %collective-permute-start.28 = (bf16[2,100,48,256]{3,2,1,0:T(8,128)(2,1)S(1)}, bf16[2,100,48,256]{3,2,1,0:T(8,128)(2,1)S(1)}, u32[]{:S(2)}, u32[]{:S(2)}) collective-permute-start(bf16[2,100,48,256]{3,2,1,0:T(8,128)(2,1)S(1)} %get-tuple-element.87), channel_id=1, source_target_pairs={{0,1},{1,2},{2,3},{4,5},{5,6},{6,7},{8,9},{9,10},{10,11},{12,13},{... | collective-permute-start | bytes 14745608 | tf_op jit(solution)/shard_map/ppermute | solution.py:26
  386.4 2.4 fusion.628
  388.8 2.5 fusion.630
  391.3 15.8 %fusion.201 = bf16[512,256]{1,0:T(8,128)(2,1)} fusion(f32[512,256]{1,0:T(8,128)} %fusion.345, f32[512,256]{1,0:T(8,128)} %fusion.346, f32[512,256]{1,0:T(8,128)} %fusion.347, f32[512,256]{1,0:T(8,128)} %fusion.348, f32[512,256]{1,0:T(8,128)} %fusion.349, f32[512,256]{1,0:T(8,128)} %fusion.350, f32[512,256]{1,0:T(8,128)} %fusion.351, ...), kind=kOutput, calls=%fused_computation.455 | convolution fusion | flops 20317184 | bytes 38278144 | tf_op jit(solution)/shard_map/dot_general | solution.py:96
  407.2 2.2 collective-permute-start.29
  416.0 14.7 %collective-permute-done.28 = bf16[2,100,48,256]{3,2,1,0:T(8,128)(2,1)S(1)} collective-permute-done((bf16[2,100,48,256]{3,2,1,0:T(8,128)(2,1)S(1)}, bf16[2,100,48,256]{3,2,1,0:T(8,128)(2,1)S(1)}, u32[]{:S(2)}, u32[]{:S(2)}) %collective-permute-start.28) | collective-permute-done | bytes 4915232 | tf_op jit(solution)/shard_map/ppermute | solution.py:26
  437.5 2.6 pad_maximum_fusion.43
  448.3 18.1 %collective-permute-done.29 = bf16[2,100,48,256]{3,2,1,0:T(8,128)(2,1)S(1)} collective-permute-done((bf16[2,100,48,256]{3,2,1,0:T(8,128)(2,1)S(1)}, bf16[2,100,48,256]{3,2,1,0:T(8,128)(2,1)S(1)}, u32[]{:S(2)}, u32[]{:S(2)}) %collective-permute-start.29) | collective-permute-done | bytes 4915232 | tf_op jit(solution)/shard_map/ppermute | solution.py:28
  470.5 2.5 pad_maximum_fusion.4
  476.4 2.5 pad_maximum_fusion.22
  514.9 2.9 pad_maximum_fusion.44
  517.8 3.0 pad_maximum_fusion.45
  520.8 3.0 pad_maximum_fusion.23
  523.9 3.0 pad_maximum_fusion.24
  527.6 9.7 %fusion.103 = bf16[512,256]{1,0:T(8,128)(2,1)} fusion(f32[512,256]{1,0:T(8,128)} %fusion.298, f32[512,256]{1,0:T(8,128)S(1)} %fusion.299, f32[512,256]{1,0:T(8,128)S(1)} %fusion.300, f32[512,256]{1,0:T(8,128)S(1)} %fusion.301, f32[512,256]{1,0:T(8,128)S(1)} %fusion.302, f32[512,256]{1,0:T(8,128)S(1)} %fusion.303, f32[512,256]{1,0:T(8,128)S(1)} %fusion.304, ...), kind=kOutput, calls=%fused_computation.309 | convolution fusion | flops 20055040 | bytes 38016000 | tf_op jit(solution)/shard_map/dot_general | solution.py:96
  (411 shorter events, 182.1 us)
Async XLA Ops:
  0.6 64.1 %copy-start.3 = (bf16[4,128,256]{2,1,0:T(8,128)(2,1)S(1)}, bf16[4,128,256]{2,1,0:T(8,128)(2,1)}, u32[]{:S(2)}) copy-start(bf16[4,128,256]{2,1,0:T(8,128)(2,1)} %param.7) | copy-start | bytes 786436
  0.6 64.1 %copy-start.2 = (bf16[4,128,256]{2,1,0:T(8,128)(2,1)S(1)}, bf16[4,128,256]{2,1,0:T(8,128)(2,1)}, u32[]{:S(2)}) copy-start(bf16[4,128,256]{2,1,0:T(8,128)(2,1)} %param.8) | copy-start | bytes 786436
  1.8 134.2 %collective-permute-start.4 = (bf16[2,4,128,256]{3,2,1,0:T(8,128)(2,1)S(1)}, bf16[2,4,128,256]{3,2,1,0:T(8,128)(2,1)S(1)}, u32[]{:S(2)}, u32[]{:S(2)}) collective-permute-start(bf16[2,4,128,256]{3,2,1,0:T(8,128)(2,1)S(1)} %pad_maximum_fusion.2), channel_id=1, source_target_pairs={{0,48},{4,52},{8,56},{12,60},{16,64},{20,68},{24,72},{28,76},{32,8... | collective-permute-start | bytes 1572872 | tf_op jit(solution)/shard_map/ppermute | solution.py:15
  5.1 134.4 %collective-permute-start.5 = (bf16[2,4,128,256]{3,2,1,0:T(8,128)(2,1)S(1)}, bf16[2,4,128,256]{3,2,1,0:T(8,128)(2,1)S(1)}, u32[]{:S(2)}, u32[]{:S(2)}) collective-permute-start(bf16[2,4,128,256]{3,2,1,0:T(8,128)(2,1)S(1)} %pad_maximum_fusion.2), channel_id=1, source_target_pairs={{0,44},{4,48},{8,52},{12,56},{16,60},{20,64},{24,68},{28,72},{32,7... | collective-permute-start | bytes 1572872 | tf_op jit(solution)/shard_map/ppermute | solution.py:15
  7.0 138.1 %collective-permute-start.6 = (bf16[2,4,128,256]{3,2,1,0:T(8,128)(2,1)S(1)}, bf16[2,4,128,256]{3,2,1,0:T(8,128)(2,1)S(1)}, u32[]{:S(2)}, u32[]{:S(2)}) collective-permute-start(bf16[2,4,128,256]{3,2,1,0:T(8,128)(2,1)S(1)} %pad_maximum_fusion.2), channel_id=1, source_target_pairs={{0,40},{4,44},{8,48},{12,52},{16,56},{20,60},{24,64},{28,68},{32,7... | collective-permute-start | bytes 1572872 | tf_op jit(solution)/shard_map/ppermute | solution.py:15
  11.4 11.9 %collective-permute-start = (bf16[2,3,128,256]{3,2,1,0:T(8,128)(2,1)}, bf16[2,3,128,256]{3,2,1,0:T(8,128)(2,1)S(1)}, u32[]{:S(2)}, u32[]{:S(2)}) collective-permute-start(bf16[2,3,128,256]{3,2,1,0:T(8,128)(2,1)} %get-tuple-element.202), channel_id=1, source_target_pairs={{0,4},{4,8},{8,12},{12,16},{16,20},{20,24},{24,28},{28,32},{32,36}... | collective-permute-start | bytes 1179656 | tf_op jit(solution)/shard_map/ppermute | solution.py:26
  14.3 11.5 %collective-permute-start.1 = (bf16[2,3,128,256]{3,2,1,0:T(8,128)(2,1)}, bf16[2,3,128,256]{3,2,1,0:T(8,128)(2,1)S(1)}, u32[]{:S(2)}, u32[]{:S(2)}) collective-permute-start(bf16[2,3,128,256]{3,2,1,0:T(8,128)(2,1)} %get-tuple-element.203), channel_id=1, source_target_pairs={{4,0},{8,4},{12,8},{16,12},{20,16},{24,20},{28,24},{32,28},{36,32}... | collective-permute-start | bytes 1179656 | tf_op jit(solution)/shard_map/ppermute | solution.py:28
  26.6 11.7 %collective-permute-start.2 = (bf16[2,10,3,256]{3,2,1,0:T(4,128)(2,1)S(1)}, bf16[2,10,3,256]{3,2,1,0:T(4,128)(2,1)S(1)}, u32[]{:S(2)}, u32[]{:S(2)}) collective-permute-start(bf16[2,10,3,256]{3,2,1,0:T(4,128)(2,1)S(1)} %get-tuple-element.175), channel_id=1, source_target_pairs={{0,1},{1,2},{2,3},{4,5},{5,6},{6,7},{8,9},{9,10},{10,11},{12,13},{... | collective-permute-start | bytes 92168 | tf_op jit(solution)/shard_map/ppermute | solution.py:26
  33.6 27.8 %collective-permute-start.3 = (bf16[2,10,3,256]{3,2,1,0:T(4,128)(2,1)S(1)}, bf16[2,10,3,256]{3,2,1,0:T(4,128)(2,1)S(1)}, u32[]{:S(2)}, u32[]{:S(2)}) collective-permute-start(bf16[2,10,3,256]{3,2,1,0:T(4,128)(2,1)S(1)} %get-tuple-element.174), channel_id=1, source_target_pairs={{1,0},{2,1},{3,2},{5,4},{6,5},{7,6},{9,8},{10,9},{11,10},{13,12},{... | collective-permute-start | bytes 92168 | tf_op jit(solution)/shard_map/ppermute | solution.py:28
  38.3 109.6 %collective-permute-start.7 = (bf16[2,4,128,256]{3,2,1,0:T(8,128)(2,1)S(1)}, bf16[2,4,128,256]{3,2,1,0:T(8,128)(2,1)S(1)}, u32[]{:S(2)}, u32[]{:S(2)}) collective-permute-start(bf16[2,4,128,256]{3,2,1,0:T(8,128)(2,1)S(1)} %pad_maximum_fusion.2), channel_id=1, source_target_pairs={{0,36},{4,40},{8,44},{12,48},{16,52},{20,56},{24,60},{28,64},{32,6... | collective-permute-start | bytes 1572872 | tf_op jit(solution)/shard_map/ppermute | solution.py:15
  61.4 89.3 %collective-permute-start.8 = (bf16[2,4,128,256]{3,2,1,0:T(8,128)(2,1)S(1)}, bf16[2,4,128,256]{3,2,1,0:T(8,128)(2,1)S(1)}, u32[]{:S(2)}, u32[]{:S(2)}) collective-permute-start(bf16[2,4,128,256]{3,2,1,0:T(8,128)(2,1)S(1)} %pad_maximum_fusion.2), channel_id=1, source_target_pairs={{0,32},{4,36},{8,40},{12,44},{16,48},{20,52},{24,56},{28,60},{32,6... | collective-permute-start | bytes 1572872 | tf_op jit(solution)/shard_map/ppermute | solution.py:15
  89.5 61.2 %copy-start.27 = (bf16[49,4,512]{2,1,0:T(4,128)(2,1)}, bf16[49,4,512]{2,1,0:T(4,128)(2,1)S(1)}, u32[]{:S(2)}) copy-start(bf16[49,4,512]{2,1,0:T(4,128)(2,1)S(1)} %divide_convert_fusion.1) | copy-start | bytes 602116
  108.0 124.5 %copy-start.4 = (bf16[4,128,256]{2,1,0:T(8,128)(2,1)S(1)}, bf16[4,128,256]{2,1,0:T(8,128)(2,1)}, u32[]{:S(2)}) copy-start(bf16[4,128,256]{2,1,0:T(8,128)(2,1)} %param.10) | copy-start | bytes 786436
  108.0 124.5 %copy-start.5 = (bf16[4,128,256]{2,1,0:T(8,128)(2,1)S(1)}, bf16[4,128,256]{2,1,0:T(8,128)(2,1)}, u32[]{:S(2)}) copy-start(bf16[4,128,256]{2,1,0:T(8,128)(2,1)} %param.11) | copy-start | bytes 786436
  136.0 216.7 %copy-start.16 = (bf16[2,4,128,256]{3,2,1,0:T(8,128)(2,1)}, bf16[2,4,128,256]{3,2,1,0:T(8,128)(2,1)S(1)}, u32[]{:S(2)}) copy-start(bf16[2,4,128,256]{3,2,1,0:T(8,128)(2,1)S(1)} %collective-permute-done.4) | copy-start | bytes 1572868
  136.0 18.5 %collective-permute-start.9 = (bf16[2,4,128,256]{3,2,1,0:T(8,128)(2,1)S(1)}, bf16[2,4,128,256]{3,2,1,0:T(8,128)(2,1)S(1)}, u32[]{:S(2)}, u32[]{:S(2)}) collective-permute-start(bf16[2,4,128,256]{3,2,1,0:T(8,128)(2,1)S(1)} %pad_maximum_fusion.2), channel_id=1, source_target_pairs={{0,28},{4,32},{8,36},{12,40},{16,44},{20,48},{24,52},{28,56},{32,6... | collective-permute-start | bytes 1572872 | tf_op jit(solution)/shard_map/ppermute | solution.py:15
  139.5 29.2 %collective-permute-start.10 = (bf16[2,4,128,256]{3,2,1,0:T(8,128)(2,1)S(1)}, bf16[2,4,128,256]{3,2,1,0:T(8,128)(2,1)S(1)}, u32[]{:S(2)}, u32[]{:S(2)}) collective-permute-start(bf16[2,4,128,256]{3,2,1,0:T(8,128)(2,1)S(1)} %pad_maximum_fusion.2), channel_id=1, source_target_pairs={{0,24},{4,28},{8,32},{12,36},{16,40},{20,44},{24,48},{28,52},{32,5... | collective-permute-start | bytes 1572872 | tf_op jit(solution)/shard_map/ppermute | solution.py:15
  145.1 33.0 %collective-permute-start.11 = (bf16[2,4,128,256]{3,2,1,0:T(8,128)(2,1)S(1)}, bf16[2,4,128,256]{3,2,1,0:T(8,128)(2,1)S(1)}, u32[]{:S(2)}, u32[]{:S(2)}) collective-permute-start(bf16[2,4,128,256]{3,2,1,0:T(8,128)(2,1)S(1)} %pad_maximum_fusion.2), channel_id=1, source_target_pairs={{0,20},{4,24},{8,28},{12,32},{16,36},{20,40},{24,44},{28,48},{32,5... | collective-permute-start | bytes 1572872 | tf_op jit(solution)/shard_map/ppermute | solution.py:15
  147.9 46.6 %collective-permute-start.12 = (bf16[2,4,128,256]{3,2,1,0:T(8,128)(2,1)S(1)}, bf16[2,4,128,256]{3,2,1,0:T(8,128)(2,1)S(1)}, u32[]{:S(2)}, u32[]{:S(2)}) collective-permute-start(bf16[2,4,128,256]{3,2,1,0:T(8,128)(2,1)S(1)} %pad_maximum_fusion.2), channel_id=1, source_target_pairs={{0,16},{4,20},{8,24},{12,28},{16,32},{20,36},{24,40},{28,44},{32,4... | collective-permute-start | bytes 1572872 | tf_op jit(solution)/shard_map/ppermute | solution.py:15
  150.7 202.1 %copy-start.18 = (bf16[2,4,128,256]{3,2,1,0:T(8,128)(2,1)}, bf16[2,4,128,256]{3,2,1,0:T(8,128)(2,1)S(1)}, u32[]{:S(2)}) copy-start(bf16[2,4,128,256]{3,2,1,0:T(8,128)(2,1)S(1)} %collective-permute-done.8) | copy-start | bytes 1572868
  150.7 47.1 %collective-permute-start.13 = (bf16[2,4,128,256]{3,2,1,0:T(8,128)(2,1)S(1)}, bf16[2,4,128,256]{3,2,1,0:T(8,128)(2,1)S(1)}, u32[]{:S(2)}, u32[]{:S(2)}) collective-permute-start(bf16[2,4,128,256]{3,2,1,0:T(8,128)(2,1)S(1)} %pad_maximum_fusion.2), channel_id=1, source_target_pairs={{0,12},{4,16},{8,20},{12,24},{16,28},{20,32},{24,36},{28,40},{32,4... | collective-permute-start | bytes 1572872 | tf_op jit(solution)/shard_map/ppermute | solution.py:15
  154.6 58.2 %collective-permute-start.14 = (bf16[2,4,128,256]{3,2,1,0:T(8,128)(2,1)S(1)}, bf16[2,4,128,256]{3,2,1,0:T(8,128)(2,1)S(1)}, u32[]{:S(2)}, u32[]{:S(2)}) collective-permute-start(bf16[2,4,128,256]{3,2,1,0:T(8,128)(2,1)S(1)} %pad_maximum_fusion.2), channel_id=1, source_target_pairs={{0,8},{4,12},{8,16},{12,20},{16,24},{20,28},{24,32},{28,36},{32,40... | collective-permute-start | bytes 1572872 | tf_op jit(solution)/shard_map/ppermute | solution.py:15
  168.7 54.0 %collective-permute-start.15 = (bf16[2,4,128,256]{3,2,1,0:T(8,128)(2,1)S(1)}, bf16[2,4,128,256]{3,2,1,0:T(8,128)(2,1)S(1)}, u32[]{:S(2)}, u32[]{:S(2)}) collective-permute-start(bf16[2,4,128,256]{3,2,1,0:T(8,128)(2,1)S(1)} %pad_maximum_fusion.2), channel_id=1, source_target_pairs={{0,4},{4,8},{8,12},{12,16},{16,20},{20,24},{24,28},{28,32},{32,36}... | collective-permute-start | bytes 1572872 | tf_op jit(solution)/shard_map/ppermute | solution.py:15
  178.2 55.1 %collective-permute-start.16 = (bf16[2,4,128,256]{3,2,1,0:T(8,128)(2,1)S(1)}, bf16[2,4,128,256]{3,2,1,0:T(8,128)(2,1)S(1)}, u32[]{:S(2)}, u32[]{:S(2)}) collective-permute-start(bf16[2,4,128,256]{3,2,1,0:T(8,128)(2,1)S(1)} %pad_maximum_fusion.2), channel_id=1, source_target_pairs={{4,0},{8,4},{12,8},{16,12},{20,16},{24,20},{28,24},{32,28},{36,32}... | collective-permute-start | bytes 1572872 | tf_op jit(solution)/shard_map/ppermute | solution.py:15
  194.5 158.3 %copy-start.20 = (bf16[2,4,128,256]{3,2,1,0:T(8,128)(2,1)}, bf16[2,4,128,256]{3,2,1,0:T(8,128)(2,1)S(1)}, u32[]{:S(2)}) copy-start(bf16[2,4,128,256]{3,2,1,0:T(8,128)(2,1)S(1)} %collective-permute-done.12) | copy-start | bytes 1572868
  194.5 41.6 %collective-permute-start.17 = (bf16[2,4,128,256]{3,2,1,0:T(8,128)(2,1)S(1)}, bf16[2,4,128,256]{3,2,1,0:T(8,128)(2,1)S(1)}, u32[]{:S(2)}, u32[]{:S(2)}) collective-permute-start(bf16[2,4,128,256]{3,2,1,0:T(8,128)(2,1)S(1)} %pad_maximum_fusion.2), channel_id=1, source_target_pairs={{8,0},{12,4},{16,8},{20,12},{24,16},{28,20},{32,24},{36,28},{40,32... | collective-permute-start | bytes 1572872 | tf_op jit(solution)/shard_map/ppermute | solution.py:15
  197.8 45.1 %collective-permute-start.18 = (bf16[2,4,128,256]{3,2,1,0:T(8,128)(2,1)S(1)}, bf16[2,4,128,256]{3,2,1,0:T(8,128)(2,1)S(1)}, u32[]{:S(2)}, u32[]{:S(2)}) collective-permute-start(bf16[2,4,128,256]{3,2,1,0:T(8,128)(2,1)S(1)} %pad_maximum_fusion.2), channel_id=1, source_target_pairs={{12,0},{16,4},{20,8},{24,12},{28,16},{32,20},{36,24},{40,28},{44,3... | collective-permute-start | bytes 1572872 | tf_op jit(solution)/shard_map/ppermute | solution.py:15
  212.7 47.7 %collective-permute-start.19 = (bf16[2,4,128,256]{3,2,1,0:T(8,128)(2,1)S(1)}, bf16[2,4,128,256]{3,2,1,0:T(8,128)(2,1)S(1)}, u32[]{:S(2)}, u32[]{:S(2)}) collective-permute-start(bf16[2,4,128,256]{3,2,1,0:T(8,128)(2,1)S(1)} %pad_maximum_fusion.2), channel_id=1, source_target_pairs={{16,0},{20,4},{24,8},{28,12},{32,16},{36,20},{40,24},{44,28},{48,3... | collective-permute-start | bytes 1572872 | tf_op jit(solution)/shard_map/ppermute | solution.py:15
  222.7 40.4 %collective-permute-start.20 = (bf16[2,4,128,256]{3,2,1,0:T(8,128)(2,1)S(1)}, bf16[2,4,128,256]{3,2,1,0:T(8,128)(2,1)S(1)}, u32[]{:S(2)}, u32[]{:S(2)}) collective-permute-start(bf16[2,4,128,256]{3,2,1,0:T(8,128)(2,1)S(1)} %pad_maximum_fusion.2), channel_id=1, source_target_pairs={{20,0},{24,4},{28,8},{32,12},{36,16},{40,20},{44,24},{48,28},{52,3... | collective-permute-start | bytes 1572872 | tf_op jit(solution)/shard_map/ppermute | solution.py:15
  233.3 50.9 %collective-permute-start.21 = (bf16[2,4,128,256]{3,2,1,0:T(8,128)(2,1)S(1)}, bf16[2,4,128,256]{3,2,1,0:T(8,128)(2,1)S(1)}, u32[]{:S(2)}, u32[]{:S(2)}) collective-permute-start(bf16[2,4,128,256]{3,2,1,0:T(8,128)(2,1)S(1)} %pad_maximum_fusion.2), channel_id=1, source_target_pairs={{24,0},{28,4},{32,8},{36,12},{40,16},{44,20},{48,24},{52,28},{56,3... | collective-permute-start | bytes 1572872 | tf_op jit(solution)/shard_map/ppermute | solution.py:15
  236.1 68.6 %collective-permute-start.22 = (bf16[2,4,128,256]{3,2,1,0:T(8,128)(2,1)S(1)}, bf16[2,4,128,256]{3,2,1,0:T(8,128)(2,1)S(1)}, u32[]{:S(2)}, u32[]{:S(2)}) collective-permute-start(bf16[2,4,128,256]{3,2,1,0:T(8,128)(2,1)S(1)} %pad_maximum_fusion.2), channel_id=1, source_target_pairs={{28,0},{32,4},{36,8},{40,12},{44,16},{48,20},{52,24},{56,28},{60,3... | collective-permute-start | bytes 1572872 | tf_op jit(solution)/shard_map/ppermute | solution.py:15
  242.9 72.8 %collective-permute-start.23 = (bf16[2,4,128,256]{3,2,1,0:T(8,128)(2,1)S(1)}, bf16[2,4,128,256]{3,2,1,0:T(8,128)(2,1)S(1)}, u32[]{:S(2)}, u32[]{:S(2)}) collective-permute-start(bf16[2,4,128,256]{3,2,1,0:T(8,128)(2,1)S(1)} %pad_maximum_fusion.2), channel_id=1, source_target_pairs={{32,0},{36,4},{40,8},{44,12},{48,16},{52,20},{56,24},{60,28},{64,3... | collective-permute-start | bytes 1572872 | tf_op jit(solution)/shard_map/ppermute | solution.py:15
  260.4 92.3 %copy-start.22 = (bf16[2,4,128,256]{3,2,1,0:T(8,128)(2,1)}, bf16[2,4,128,256]{3,2,1,0:T(8,128)(2,1)S(1)}, u32[]{:S(2)}) copy-start(bf16[2,4,128,256]{3,2,1,0:T(8,128)(2,1)S(1)} %collective-permute-done.19) | copy-start | bytes 1572868
  260.4 56.2 %collective-permute-start.24 = (bf16[2,4,128,256]{3,2,1,0:T(8,128)(2,1)S(1)}, bf16[2,4,128,256]{3,2,1,0:T(8,128)(2,1)S(1)}, u32[]{:S(2)}, u32[]{:S(2)}) collective-permute-start(bf16[2,4,128,256]{3,2,1,0:T(8,128)(2,1)S(1)} %pad_maximum_fusion.2), channel_id=1, source_target_pairs={{36,0},{40,4},{44,8},{48,12},{52,16},{56,20},{60,24},{64,28},{68,3... | collective-permute-start | bytes 1572872 | tf_op jit(solution)/shard_map/ppermute | solution.py:15
  263.1 54.4 %collective-permute-start.25 = (bf16[2,4,128,256]{3,2,1,0:T(8,128)(2,1)S(1)}, bf16[2,4,128,256]{3,2,1,0:T(8,128)(2,1)S(1)}, u32[]{:S(2)}, u32[]{:S(2)}) collective-permute-start(bf16[2,4,128,256]{3,2,1,0:T(8,128)(2,1)S(1)} %pad_maximum_fusion.2), channel_id=1, source_target_pairs={{40,0},{44,4},{48,8},{52,12},{56,16},{60,20},{64,24},{68,28},{72,3... | collective-permute-start | bytes 1572872 | tf_op jit(solution)/shard_map/ppermute | solution.py:15
  284.2 38.3 %collective-permute-start.26 = (bf16[2,4,128,256]{3,2,1,0:T(8,128)(2,1)S(1)}, bf16[2,4,128,256]{3,2,1,0:T(8,128)(2,1)S(1)}, u32[]{:S(2)}, u32[]{:S(2)}) collective-permute-start(bf16[2,4,128,256]{3,2,1,0:T(8,128)(2,1)S(1)} %pad_maximum_fusion.2), channel_id=1, source_target_pairs={{44,0},{48,4},{52,8},{56,12},{60,16},{64,20},{68,24},{72,28},{76,3... | collective-permute-start | bytes 1572872 | tf_op jit(solution)/shard_map/ppermute | solution.py:15
  304.7 48.0 %collective-permute-start.27 = (bf16[2,4,128,256]{3,2,1,0:T(8,128)(2,1)S(1)}, bf16[2,4,128,256]{3,2,1,0:T(8,128)(2,1)S(1)}, u32[]{:S(2)}, u32[]{:S(2)}) collective-permute-start(bf16[2,4,128,256]{3,2,1,0:T(8,128)(2,1)S(1)} %pad_maximum_fusion.2), channel_id=1, source_target_pairs={{48,0},{52,4},{56,8},{60,12},{64,16},{68,20},{72,24},{76,28},{80,3... | collective-permute-start | bytes 1572872 | tf_op jit(solution)/shard_map/ppermute | solution.py:15
  315.7 37.0 %copy-start.24 = (bf16[2,4,128,256]{3,2,1,0:T(8,128)(2,1)}, bf16[2,4,128,256]{3,2,1,0:T(8,128)(2,1)S(1)}, u32[]{:S(2)}) copy-start(bf16[2,4,128,256]{3,2,1,0:T(8,128)(2,1)S(1)} %collective-permute-done.23) | copy-start | bytes 1572868
  361.5 69.3 %collective-permute-start.28 = (bf16[2,100,48,256]{3,2,1,0:T(8,128)(2,1)S(1)}, bf16[2,100,48,256]{3,2,1,0:T(8,128)(2,1)S(1)}, u32[]{:S(2)}, u32[]{:S(2)}) collective-permute-start(bf16[2,100,48,256]{3,2,1,0:T(8,128)(2,1)S(1)} %get-tuple-element.87), channel_id=1, source_target_pairs={{0,1},{1,2},{2,3},{4,5},{5,6},{6,7},{8,9},{9,10},{10,11},{12,13},{... | collective-permute-start | bytes 14745608 | tf_op jit(solution)/shard_map/ppermute | solution.py:26
  407.2 25.0 %copy-start.1 = (bf16[4,128,256]{2,1,0:T(8,128)(2,1)S(1)}, bf16[4,128,256]{2,1,0:T(8,128)(2,1)}, u32[]{:S(2)}) copy-start(bf16[4,128,256]{2,1,0:T(8,128)(2,1)} %param.9) | copy-start | bytes 786436
  407.2 25.0 %copy-start.53 = (pred[512]{0:T(512)(128)(4,1)S(1)}, pred[512]{0:T(512)(128)(4,1)}, u32[]{:S(2)}) copy-start(pred[512]{0:T(512)(128)(4,1)} %get-tuple-element.300) | copy-start | bytes 1540
  407.2 25.4 %copy-start.52 = (pred[512]{0:T(512)(128)(4,1)S(1)}, pred[512]{0:T(512)(128)(4,1)}, u32[]{:S(2)}) copy-start(pred[512]{0:T(512)(128)(4,1)} %get-tuple-element.313) | copy-start | bytes 1540
  407.2 59.2 %collective-permute-start.29 = (bf16[2,100,48,256]{3,2,1,0:T(8,128)(2,1)S(1)}, bf16[2,100,48,256]{3,2,1,0:T(8,128)(2,1)S(1)}, u32[]{:S(2)}, u32[]{:S(2)}) collective-permute-start(bf16[2,100,48,256]{3,2,1,0:T(8,128)(2,1)S(1)} %bitcast.1268), channel_id=1, source_target_pairs={{1,0},{2,1},{3,2},{5,4},{6,5},{7,6},{9,8},{10,9},{11,10},{13,12},{... | collective-permute-start | bytes 14745608 | tf_op jit(solution)/shard_map/ppermute | solution.py:28
  410.2 23.2 %copy-start.56 = (pred[512]{0:T(512)(128)(4,1)S(1)}, pred[512]{0:T(512)(128)(4,1)}, u32[]{:S(2)}) copy-start(pred[512]{0:T(512)(128)(4,1)} %get-tuple-element.272) | copy-start | bytes 1540
  411.0 23.3 %copy-start.54 = (pred[512]{0:T(512)(128)(4,1)S(1)}, pred[512]{0:T(512)(128)(4,1)}, u32[]{:S(2)}) copy-start(pred[512]{0:T(512)(128)(4,1)} %get-tuple-element.257) | copy-start | bytes 1540
  444.6 24.6 %copy-start.29 = (pred[512]{0:T(512)(128)(4,1)S(1)}, pred[512]{0:T(512)(128)(4,1)}, u32[]{:S(2)}) copy-start(pred[512]{0:T(512)(128)(4,1)} %get-tuple-element.275) | copy-start | bytes 1540
  481.8 32.0 %copy-start.6 = (bf16[4,128,256]{2,1,0:T(8,128)(2,1)S(1)}, bf16[4,128,256]{2,1,0:T(8,128)(2,1)}, u32[]{:S(2)}) copy-start(bf16[4,128,256]{2,1,0:T(8,128)(2,1)} %param.11) | copy-start | bytes 786436
  482.2 31.6 %copy-start.28 = (bf16[49,4,512]{2,1,0:T(4,128)(2,1)}, bf16[49,4,512]{2,1,0:T(4,128)(2,1)S(1)}, u32[]{:S(2)}) copy-start(bf16[49,4,512]{2,1,0:T(4,128)(2,1)S(1)} %divide_convert_fusion) | copy-start | bytes 602116
  (41 other events, 333.6 us)
where the time goes:
time: 542 us; the launch traced here: 538 us
  starting transfers between devices  201 us (37%)
  matrix products  154 us (28%)
  waiting for transfers between devices  101 us (19%)
  local copies, waits for them, and re-layouts  44.9 us (8%)
  other arithmetic  34.3 us (6%)
    ppermute x24, starting transfers between devices, passed_along(): return lax.ppermute(block, axis, route)  169 us
    dot_general x98, matrix products, window_attend(): lax.dot_general(probs[position], table_narrow, head_spread, preferred_ele...  113 us
    ppermute x24, waiting for transfers between devices, passed_along(): return lax.ppermute(block, axis, route)  61.2 us
    dot_general x98, matrix products, window_attend(): lax.dot_general(table_wide, product, head_sum, precision=lax.Precision.HI...  40.2 us
    ppermute x3, starting transfers between devices, with_halo(): lax.ppermute(tail, axis, [(i, (i + 1) % count) for i in range(ends)])  26 us
    unnamed x141, local copies, waits for them, and re-layouts  21.1 us
    ppermute x3, waiting for transfers between devices, with_halo(): lax.ppermute(head, axis, [((i + 1) % count, i) for i in range(ends)])  20.6 us
    ppermute x3, waiting for transfers between devices, with_halo(): lax.ppermute(tail, axis, [(i, (i + 1) % count) for i in range(ends)])  19.2 us
  transfers between devices with their start and end apart: 30, of which 10 were waited for; matrix products, arithmetic and copies ran while one was open for 28% of the time, Pallas kernels for 0%

commit v1 on v0

v1 whole, which is shorter than its diff:
```python
import functools
import math

import jax
import jax.numpy as jnp
from jax import lax
from jax.experimental import pallas as pl
from jax.experimental.pallas import tpu as pltpu
from jax.sharding import PartitionSpec as P

MESH = pl.DeviceIdType.MESH
HEADS = 4
HEAD = 64
CH = 256
ROWS = 4
COLS = 128
STRIP = 48
WIDE = COLS + 2 * STRIP
STEP = 16
SLOTS = 7
OWN = 3
EDGE = 16
NEAR_WIDE = COLS + 2 * EDGE
NEAR_ROWS = ROWS + 6
TILE = 32
TILES = COLS // TILE
KEYS = TILE + 2 * STRIP
NEAR_KEYS = TILE + 2 * EDGE
SCALE = math.log2(math.e) / math.sqrt(HEAD)
NONE = 99

SECOND = (
    (1, -1, -1, NONE, 1, -2, NONE, NONE),
    (NONE, NONE, 2, -1, NONE, 1, 1, -1),
    (4, 2, 2, 2, -2, -2, -2, -4),
)
FROM_STREAM = ((2, 2, 0, 0, 2, 0, 0, 0), (0, 0, 1, 2, 0, 1, 2, 2), (1, 1, 1, 1, 0, 0, 0, 0))
FROM_SECOND = ((0, 0, 1, 0, 0, 0, 0, 0), (0, 0, 0, 0, 0, 1, 0, 0), (1, 0, 0, 0, 0, 0, 0, 1))
VALUES_LAST = ((0, 5), (2, 7), ())


def pick(table, place):
    out = jnp.int32(table[0])
    for k in range(1, len(table)):
        out = jnp.where(place == k, jnp.int32(table[k]), out)
    return out


def one_of(place, places):
    out = jnp.bool_(False)
    for k in places:
        out = out | (place == k)
    return out


def kernel(
    qn_ref, kn_ref, vn_ref, qf_ref, kf_ref, vf_ref, on_ref, of_ref,
    far, near, qn, qf, qb, scores, peak, probs, total, acc, bias_far, bias_near, out_near, out_far,
    load_sem, far_send, far_recv, strip_send, strip_recv, side_send, side_recv, near_send, near_recv, out_sem,
):
    row = lax.axis_index("row")
    col = lax.axis_index("col")
    n_rows = lax.axis_size("row")
    n_cols = lax.axis_size("col")
    x = row // 8
    z = (row // 4) % 2
    core = col % 2
    place = 2 * x + z
    inner = (col == 1) | (col == 2)
    true = jnp.bool_(True)

    loads = [
        pltpu.make_async_copy(kf_ref, far.at[0, OWN, :, pl.ds(STRIP, COLS)], load_sem.at[0]),
        pltpu.make_async_copy(vf_ref, far.at[1, OWN, :, pl.ds(STRIP, COLS)], load_sem.at[1]),
        pltpu.make_async_copy(kn_ref, near.at[0, pl.ds(3, ROWS), pl.ds(EDGE, COLS)], load_sem.at[2]),
        pltpu.make_async_copy(vn_ref, near.at[1, pl.ds(3, ROWS), pl.ds(EDGE, COLS)], load_sem.at[3]),
        pltpu.make_async_copy(qf_ref, qf, load_sem.at[4]),
        pltpu.make_async_copy(qn_ref, qn, load_sem.at[5]),
    ]
    for load in loads:
        load.start()

    to_row = (row + 8, row - 8, row + 4 - 8 * z)
    first_send = (x < 3, x > 0, true)
    first_recv = (x > 0, x < 3, true)
    first_to = (jnp.int32(1), jnp.int32(5), 2 + 2 * z)
    first_in = (jnp.int32(1), jnp.int32(5), 4 - 2 * z)
    shift = (-2, 2, 2 * z - 1)
    second_rel = [pick(SECOND[s], place) for s in range(3)]
    second_send = [second_rel[s] != NONE for s in range(3)]
    second_src = [(second_rel[s] + 10) % 7 for s in range(3)]
    second_to = [(second_rel[s] + 10 + shift[s]) % 7 for s in range(3)]
    sender_place = (place - 2, place + 2, place + 1 - 2 * z)
    sender_rel = [pick(SECOND[s], sender_place[s]) for s in range(3)]
    second_recv = [first_recv[s] & (sender_rel[s] != NONE) for s in range(3)]
    second_in = [
        (sender_rel[s] + 10 + (-2, 2, 1 - 2 * z)[s]) % 7 for s in range(3)
    ]
    send_ok = (first_send, second_send)
    recv_ok = (first_recv, second_recv)
    src_slot = ((jnp.int32(OWN),) * 3, second_src)
    dst_slot = (first_to, second_to)
    in_slot = (first_in, second_in)
    values_last = [one_of(place, VALUES_LAST[s]) for s in range(3)]
    late_in = [first_recv[s] & one_of(sender_place[s], VALUES_LAST[s]) for s in range(3)]
    outer_col = jnp.where(col == 1, STRIP + COLS, 0)

    def part_cols(part):
        if part == 0:
            return pl.ds(STRIP, COLS)
        return pl.ds(pl.multiple_of(outer_col, 16), STRIP)

    def far_copy(s, o, kv, part):
        where = part_cols(part)
        return pltpu.make_async_remote_copy(
            far.at[kv, src_slot[o][s], :, where],
            far.at[kv, dst_slot[o][s], :, where],
            far_send.at[s, o, kv, part],
            far_recv.at[s, o, kv, part],
            device_id=(to_row[s], col),
            device_id_type=MESH,
        )

    def far_arrival(s, o, kv, part):
        where = part_cols(part)
        block = far.at[kv, in_slot[o][s], :, where]
        return pltpu.make_async_remote_copy(
            block, block, far_send.at[s, o, kv, part], far_recv.at[s, o, kv, part],
            device_id=(to_row[s], col), device_id_type=MESH,
        )

    def send_far(s, o, kv, ok=true, parts=(0, 1)):
        for part in parts:
            good = send_ok[o][s] & ok
            if part == 1:
                good = good & inner

            @pl.when(good)
            def _():
                far_copy(s, o, kv, part).start()

    def wait_far(s, o, kv, ok=true):
        for part in (0, 1):
            good = recv_ok[o][s] & ok
            if part == 1:
                good = good & inner

            @pl.when(good)
            def _():
                far_arrival(s, o, kv, part).wait_recv()

    mate = col + 1 - 2 * core
    strip_src = pl.multiple_of(jnp.where(core == 0, COLS, STRIP), 16)
    strip_dst = pl.multiple_of(jnp.where(core == 0, 0, STRIP + COLS), 16)
    strip_in = pl.multiple_of(jnp.where(core == 0, STRIP + COLS, 0), 16)

    def strip_copy(e, kv, slot):
        return pltpu.make_async_remote_copy(
            far.at[kv, slot, :, pl.ds(strip_src, STRIP)],
            far.at[kv, slot, :, pl.ds(strip_dst, STRIP)],
            strip_send.at[e, kv],
            strip_recv.at[e, kv],
            device_id=(row, mate),
            device_id_type=MESH,
        )

    def strip_arrival(e, kv, slot):
        block = far.at[kv, slot, :, pl.ds(strip_in, STRIP)]
        return pltpu.make_async_remote_copy(
            block, block, strip_send.at[e, kv], strip_recv.at[e, kv],
            device_id=(row, mate), device_id_type=MESH,
        )

    def send_strip(s, o, kv, ok=true):
        @pl.when(recv_ok[o][s] & ok)
        def _():
            strip_copy(1 + 3 * o + s, kv, in_slot[o][s]).start()

    def wait_strip(s, o, kv):
        @pl.when(recv_ok[o][s])
        def _():
            strip_arrival(1 + 3 * o + s, kv, in_slot[o][s]).wait_recv()

    side_src = pl.multiple_of(jnp.where(col == 1, COLS, STRIP), 16)
    side_dst = pl.multiple_of(jnp.where(col == 1, 0, STRIP + COLS), 16)

    def side_copy(kv):
        return pltpu.make_async_remote_copy(
            far.at[kv, OWN, :, pl.ds(side_src, STRIP)],
            far.at[kv, OWN, :, pl.ds(side_dst, STRIP)],
            side_send.at[kv],
            side_recv.at[kv],
            device_id=(row, 3 - col),
            device_id_type=MESH,
        )

    def side_arrival(kv):
        block = far.at[kv, OWN, :, part_cols(1)]
        return pltpu.make_async_remote_copy(
            block, block, side_send.at[kv], side_recv.at[kv], device_id=(row, 3 - col), device_id_type=MESH
        )

    sides = [(dr, dc) for dr in (-1, 0, 1) for dc in (-1, 0, 1) if (dr, dc) != (0, 0)]

    def there(dr, dc):
        good = true
        if dr:
            good = good & ((row + dr >= 0) & (row + dr < n_rows))
        if dc:
            good = good & ((col + dc >= 0) & (col + dc < n_cols))
        return good

    row_src = {1: (4, 3), -1: (3, 3), 0: (3, ROWS)}
    row_dst = {1: (0, 3), -1: (7, 3), 0: (3, ROWS)}
    col_src = {1: (COLS, EDGE), -1: (EDGE, EDGE), 0: (EDGE, COLS)}
    col_dst = {1: (0, EDGE), -1: (EDGE + COLS, EDGE), 0: (EDGE, COLS)}

    def near_copy(n, kv):
        dr, dc = sides[n]
        return pltpu.make_async_remote_copy(
            near.at[kv, pl.ds(*row_src[dr]), pl.ds(*col_src[dc])],
            near.at[kv, pl.ds(*row_dst[dr]), pl.ds(*col_dst[dc])],
            near_send.at[n, kv],
            near_recv.at[n, kv],
            device_id=(row + dr, col + dc),
            device_id_type=MESH,
        )

    def near_arrival(n, kv):
        dr, dc = sides[n]
        block = near.at[kv, pl.ds(*row_dst[dr]), pl.ds(*col_dst[dc])]
        return pltpu.make_async_remote_copy(
            block, block, near_send.at[n, kv], near_recv.at[n, kv],
            device_id=(row - dr, col - dc), device_id_type=MESH,
        )

    barrier = pltpu.get_barrier_semaphore()
    expected = jnp.int32(0)
    for s in range(3):
        @pl.when(first_send[s])
        def _():
            pl.semaphore_signal(barrier, inc=1, device_id=(to_row[s], col), device_id_type=MESH)

        expected = expected + first_recv[s].astype(jnp.int32)
    for dr, dc in sides:
        @pl.when(there(dr, dc))
        def _():
            pl.semaphore_signal(barrier, inc=1, device_id=(row + dr, col + dc), device_id_type=MESH)

        expected = expected + there(-dr, -dc).astype(jnp.int32)
    pl.semaphore_wait(barrier, expected)

    loads[0].wait()
    for s in range(3):
        send_far(s, 0, 0, parts=(0,))
    strip_copy(0, 0, OWN).start()

    @pl.when(inner)
    def _():
        side_copy(0).start()

    loads[1].wait()

    @pl.when(inner)
    def _():
        side_copy(1).start()

    for s in range(3):
        send_far(s, 0, 1, ok=~values_last[s], parts=(0,))
    strip_copy(0, 1, OWN).start()
    loads[2].wait()
    loads[3].wait()
    for n, (dr, dc) in enumerate(sides):
        @pl.when(there(dr, dc))
        def _():
            near_copy(n, 0).start()
            near_copy(n, 1).start()

    c0 = col * COLS
    width = n_cols * COLS
    for t in range(TILES):
        q_at = lax.broadcasted_iota(jnp.int32, (TILE, KEYS), 0)
        k_at = lax.broadcasted_iota(jnp.int32, (TILE, KEYS), 1)
        apart = k_at - q_at
        k_col = c0 + TILE * t - STRIP + k_at
        good = ((apart & (STEP - 1)) == 0) & (apart >= 0) & (apart <= 2 * STRIP) & (k_col >= 0) & (k_col < width)
        bias_far[t] = jnp.where(good, 0.0, -jnp.inf)
    for rp in range(2):
        for t in range(TILES):
            shape = (2, TILE, 8, NEAR_KEYS)
            shape = (2 * TILE, 8 * NEAR_KEYS)
            q_id = lax.broadcasted_iota(jnp.int32, shape, 0)
            k_id = lax.broadcasted_iota(jnp.int32, shape, 1)
            r_off = (k_id // NEAR_KEYS) - (q_id // TILE)
            c_off = (k_id % NEAR_KEYS) - (q_id % TILE) - EDGE
            k_row = row * ROWS + 2 * rp - 3 + (k_id // NEAR_KEYS)
            k_col = c0 + TILE * t - EDGE + (k_id % NEAR_KEYS)
            good = (r_off >= 0) & (r_off <= 6) & (c_off >= -3) & (c_off <= 3)
            good = good & (k_row >= 0) & (k_row < n_rows * ROWS) & (k_col >= 0) & (k_col < width)
            bias_near[rp * TILES + t] = jnp.where(good, 0.0, -jnp.inf)

    zero = lambda shape: jnp.zeros(shape, jnp.bfloat16)
    for a in range(SLOTS):
        relayed = (a == 0) & (place == 0) | (a == 6) & (place == 7)
        lost = ((place + a - OWN < 0) | (place + a - OWN > 7)) & ~relayed

        @pl.when(lost)
        def _():
            for kv in range(2):
                for r in range(ROWS):
                    far[kv, a, r] = zero((WIDE, CH))

        @pl.when(~lost & (col == 0))
        def _():
            for kv in range(2):
                for r in range(ROWS):
                    far[kv, a, r, 0:STRIP] = zero((STRIP, CH))

        @pl.when(~lost & (col == 3))
        def _():
            for kv in range(2):
                for r in range(ROWS):
                    far[kv, a, r, STRIP + COLS : WIDE] = zero((STRIP, CH))

    for kv in range(2):
        @pl.when(row == 0)
        def _():
            near[kv, 0:3] = zero((3, NEAR_WIDE, CH))

        @pl.when(row == n_rows - 1)
        def _():
            near[kv, 7:10] = zero((3, NEAR_WIDE, CH))

        @pl.when(col == 0)
        def _():
            near[kv, :, 0:EDGE] = zero((NEAR_ROWS, EDGE, CH))

        @pl.when(col == n_cols - 1)
        def _():
            near[kv, :, EDGE + COLS : NEAR_WIDE] = zero((NEAR_ROWS, EDGE, CH))

    lane_head = lax.broadcasted_iota(jnp.int32, (1, CH), 1) // HEAD
    head_mask = [(lane_head == h).astype(jnp.float32) for h in range(HEADS)]
    head_mask_narrow = [m.astype(jnp.bfloat16) for m in head_mask]
    dims_t = (((1,), (1,)), ((), ()))
    dims = (((1,), (0,)), ((), ()))

    loads[4].wait()
    loads[5].wait()

    def block_queries(q):
        return jnp.concatenate([q * head_mask_narrow[h] for h in range(HEADS)], axis=0)

    @pl.loop(0, ROWS)
    def _(r):
        for t in range(TILES):
            qb[r * TILES + t] = block_queries(qf[r, TILE * t : TILE * (t + 1), :])

    def score_block(slot, first=False):
        ok = (place + slot - OWN >= 0) & (place + slot - OWN <= 7)
        row_bias = jnp.where(ok, 0.0, -jnp.inf).astype(jnp.float32)

        @pl.loop(0, ROWS)
        def _(r):
            for t in range(TILES):
                idx = r * TILES + t
                k = far[0, slot, r, TILE * t : TILE * t + KEYS, :]
                s = lax.dot_general(qb[idx], k, dims_t, preferred_element_type=jnp.float32) * SCALE
                b = bias_far[t] + row_bias
                s = s.reshape(HEADS, TILE, KEYS) + b[None]
                s = s.reshape(HEADS * TILE, KEYS)
                scores[slot, idx] = s
                peak[idx] = s if first else jnp.maximum(peak[idx], s)

    def value_blocks(slots, first=False):
        @pl.loop(0, ROWS)
        def _(r):
            for t in range(TILES):
                idx = r * TILES + t
                o = None if first else acc[idx]
                for slot in slots:
                    v = far[1, slot, r, TILE * t : TILE * t + KEYS, :]
                    d = lax.dot_general(probs[slot, idx], v, dims, preferred_element_type=jnp.float32)
                    o = d if o is None else o + d
                acc[idx] = o

    strip_arrival(0, 0, OWN).wait_recv()

    @pl.when(inner)
    def _():
        side_arrival(0).wait_recv()

    for s in range(3):
        send_far(s, 0, 0, parts=(1,))

    @pl.when(inner)
    def _():
        side_arrival(1).wait_recv()

    for s in range(3):
        send_far(s, 0, 1, ok=~values_last[s], parts=(1,))
    score_block(OWN, first=True)

    from_stream = [pick(FROM_STREAM[s], place) for s in range(3)]
    after_first = [pick(FROM_SECOND[s], place) == 0 for s in range(3)]
    needs_second = [jnp.bool_(False)] * 3
    for s in range(3):
        for d in range(3):
            needs_second[d] = needs_second[d] | (second_send[s] & ~after_first[s] & (from_stream[s] == d))

    for s in range(3):
        wait_far(s, 0, 0)
    for s in range(3):
        send_far(s, 1, 0, ok=after_first[s])
    for s in range(3):
        send_strip(s, 0, 0)
    for s in range(3):
        wait_strip(s, 0, 0)
    for s in range(3):
        score_block(first_in[s])

    for s in range(3):
        wait_far(s, 0, 1, ok=~late_in[s])
    for s in range(3):
        send_far(s, 1, 1, ok=after_first[s])
    for s in range(3):
        send_far(s, 0, 1, ok=values_last[s])
    for s in range(3):
        wait_far(s, 1, 0, ok=needs_second[s])
    for s in range(3):
        send_far(s, 1, 0, ok=~after_first[s])
    for s in range(3):
        send_strip(s, 0, 1, ok=~late_in[s])

    for n, (dr, dc) in enumerate(sides):
        @pl.when(there(-dr, -dc))
        def _():
            near_arrival(n, 0).wait_recv()
            near_arrival(n, 1).wait_recv()

    @pl.loop(0, 2)
    def _(rp):
        for t in range(TILES):
            q = qn[pl.ds(2 * rp, 2), TILE * t : TILE * (t + 1), :].reshape(2 * TILE, CH)
            k = near[0, pl.ds(2 * rp, 8), TILE * t : TILE * t + NEAR_KEYS, :].reshape(8 * NEAR_KEYS, CH)
            v = near[1, pl.ds(2 * rp, 8), TILE * t : TILE * t + NEAR_KEYS, :].reshape(8 * NEAR_KEYS, CH)
            b = bias_near[rp * TILES + t]
            out = None
            for h in range(HEADS):
                s = lax.dot_general(q * head_mask_narrow[h], k, dims_t, preferred_element_type=jnp.float32)
                s = s * SCALE + b
                p = jnp.exp2(s - jnp.max(s, axis=1, keepdims=True))
                o = lax.dot_general(p.astype(jnp.bfloat16), v, dims, preferred_element_type=jnp.float32)
                o = o * (head_mask[h] / jnp.sum(p, axis=1, keepdims=True))
                out = o if out is None else out + o
            out_near[pl.ds(2 * rp, 2), TILE * t : TILE * (t + 1), :] = out.astype(jnp.bfloat16).reshape(2, TILE, CH)

    near_out = pltpu.make_async_copy(out_near, on_ref, out_sem.at[0])
    near_out.start()

    for s in range(3):
        wait_far(s, 1, 1, ok=needs_second[s])
    for s in range(3):
        send_far(s, 1, 1, ok=~after_first[s])
    for s in range(3):
        wait_far(s, 1, 0, ok=~needs_second[s])
    for s in range(3):
        send_strip(s, 1, 0)
    for s in range(3):
        wait_strip(s, 1, 0)
    second_slots = (jnp.int32(0), jnp.int32(6), 2 + 2 * z)
    for s in range(3):
        score_block(second_slots[s])

    @pl.loop(0, ROWS)
    def _(r):
        for t in range(TILES):
            idx = r * TILES + t
            m = jnp.max(peak[idx], axis=1, keepdims=True)
            summed = None
            for a in range(SLOTS):
                p = jnp.exp2(scores[a, idx] - m)
                probs[a, idx] = p.astype(jnp.bfloat16)
                summed = p if summed is None else summed + p
            total[idx] = jnp.broadcast_to(1.0 / jnp.sum(summed, axis=1, keepdims=True), (HEADS * TILE, 128))

    strip_arrival(0, 1, OWN).wait_recv()
    value_blocks((OWN,), first=True)
    for s in range(3):
        wait_far(s, 0, 1, ok=late_in[s])
        send_strip(s, 0, 1, ok=late_in[s])
    for s in range(3):
        wait_far(s, 1, 1, ok=~needs_second[s])
        send_strip(s, 1, 1)
    for s in range(3):
        wait_strip(s, 0, 1)
    value_blocks(first_in)
    for s in range(3):
        wait_strip(s, 1, 1)
    value_blocks(second_slots)

    @pl.loop(0, ROWS)
    def _(r):
        for t in range(TILES):
            idx = r * TILES + t
            out = None
            for h in range(HEADS):
                part = slice(h * TILE, (h + 1) * TILE)
                inverse = total[idx, part, :]
                o = acc[idx, part, :] * jnp.concatenate([inverse, inverse], axis=1) * head_mask[h]
                out = o if out is None else out + o
            out_far[r, TILE * t : TILE * (t + 1), :] = out.astype(jnp.bfloat16)

    far_out = pltpu.make_async_copy(out_far, of_ref, out_sem.at[1])
    far_out.start()

    for o in range(2):
        for s in range(3):
            for kv in range(2):
                for part in (0, 1):
                    @pl.when((send_ok[o][s] & inner) if part else send_ok[o][s])
                    def _():
                        far_copy(s, o, kv, part).wait_send()

                @pl.when(recv_ok[o][s])
                def _():
                    strip_copy(1 + 3 * o + s, kv, in_slot[o][s]).wait_send()

    for kv in range(2):
        strip_copy(0, kv, OWN).wait_send()

        @pl.when(inner)
        def _():
            side_copy(kv).wait_send()

    for n, (dr, dc) in enumerate(sides):
        @pl.when(there(dr, dc))
        def _():
            near_copy(n, 0).wait_send()
            near_copy(n, 1).wait_send()

    near_out.wait()
    far_out.wait()


def per_device(query_near, key_near, value_near, dilated_queries, dilated_keys, dilated_values):
    block = jax.ShapeDtypeStruct((ROWS, COLS, CH), jnp.bfloat16)
    tiles = ROWS * TILES
    dma = pltpu.SemaphoreType.DMA
    anywhere = pl.BlockSpec(memory_space=pl.ANY)
    return pl.pallas_call(
        kernel,
        out_shape=(block, block),
        in_specs=[anywhere] * 6,
        out_specs=(anywhere, anywhere),
        scratch_shapes=[
            pltpu.VMEM((2, SLOTS, ROWS, WIDE, CH), jnp.bfloat16),
            pltpu.VMEM((2, NEAR_ROWS, NEAR_WIDE, CH), jnp.bfloat16),
            pltpu.VMEM((ROWS, COLS, CH), jnp.bfloat16),
            pltpu.VMEM((ROWS, COLS, CH), jnp.bfloat16),
            pltpu.VMEM((tiles, HEADS * TILE, CH), jnp.bfloat16),
            pltpu.VMEM((SLOTS, tiles, HEADS * TILE, KEYS), jnp.float32),
            pltpu.VMEM((tiles, HEADS * TILE, KEYS), jnp.float32),
            pltpu.VMEM((SLOTS, tiles, HEADS * TILE, KEYS), jnp.bfloat16),
            pltpu.VMEM((tiles, HEADS * TILE, 128), jnp.float32),
            pltpu.VMEM((tiles, HEADS * TILE, CH), jnp.float32),
            pltpu.VMEM((TILES, TILE, KEYS), jnp.float32),
            pltpu.VMEM((2 * TILES, 2 * TILE, 8 * NEAR_KEYS), jnp.float32),
            pltpu.VMEM((ROWS, COLS, CH), jnp.bfloat16),
            pltpu.VMEM((ROWS, COLS, CH), jnp.bfloat16),
            dma((6,)),
            dma((3, 2, 2, 2)),
            dma((3, 2, 2, 2)),
            dma((7, 2)),
            dma((7, 2)),
            dma((2,)),
            dma((2,)),
            dma((8, 2)),
            dma((8, 2)),
            dma((2,)),
        ],
        compiler_params=pltpu.CompilerParams(
            collective_id=0, has_side_effects=True, vmem_limit_bytes=48 << 20
        ),
        name="two_layers",
    )(query_near, key_near, value_near, dilated_queries, dilated_keys, dilated_values)


def solution(mesh):
    placed = (P("row", "col", None),) * 6
    return jax.shard_map(
        per_device,
        mesh=mesh,
        in_specs=placed,
        out_specs=(P("row", "col", None), P("row", "col", None)),
        check_vma=False,
    )
```

time: 542 us -> 72 us (0.13)
  the two profiles are of different devices: /device:TPU:43 before, /device:TPU:1 now
where the time goes in v1:
time: 72 us; the launch traced here: 71.7 us
  Pallas kernels  64 us (89%)
  local copies, waits for them, and re-layouts  7.1 us (10%)
    pallas_call x1, Pallas kernels, per_device(): pl.pallas_call(kernel, out_shape=(block, block), in_specs=[anywhere] * 6,...  64 us
    unnamed x14, local copies, waits for them, and re-layouts  7.1 us

profile of v1, /device:TPU:1, one launch (start us, length us, event | category | flops | bytes accessed | tf_op | source)
XLA Modules:
  0.0 71.7 jit_solution(9165070998602538123)
XLA Ops:
  0.6 0.0 copy-start
  0.6 0.9 %copy-done = bf16[4,128,256]{2,1,0:T(8,128)(2,1)S(1)} copy-done((bf16[4,128,256]{2,1,0:T(8,128)(2,1)S(1)}, bf16[4,128,256]{2,1,0:T(8,128)(2,1)}, u32[]{:S(2)}) %copy-start) | copy-done | bytes 262168
  1.6 0.0 copy-start.1
  1.6 0.9 %copy-done.1 = bf16[4,128,256]{2,1,0:T(8,128)(2,1)S(1)} copy-done((bf16[4,128,256]{2,1,0:T(8,128)(2,1)S(1)}, bf16[4,128,256]{2,1,0:T(8,128)(2,1)}, u32[]{:S(2)}) %copy-start.1) | copy-done | bytes 262168
  2.5 0.0 copy-start.2
  2.5 0.9 %copy-done.2 = bf16[4,128,256]{2,1,0:T(8,128)(2,1)S(1)} copy-done((bf16[4,128,256]{2,1,0:T(8,128)(2,1)S(1)}, bf16[4,128,256]{2,1,0:T(8,128)(2,1)}, u32[]{:S(2)}) %copy-start.2) | copy-done | bytes 262168
  3.5 0.0 copy-start.3
  3.5 0.9 %copy-done.3 = bf16[4,128,256]{2,1,0:T(8,128)(2,1)S(1)} copy-done((bf16[4,128,256]{2,1,0:T(8,128)(2,1)S(1)}, bf16[4,128,256]{2,1,0:T(8,128)(2,1)}, u32[]{:S(2)}) %copy-start.3) | copy-done | bytes 262168
  4.4 0.0 copy-start.4
  4.4 0.9 %copy-done.4 = bf16[4,128,256]{2,1,0:T(8,128)(2,1)S(1)} copy-done((bf16[4,128,256]{2,1,0:T(8,128)(2,1)S(1)}, bf16[4,128,256]{2,1,0:T(8,128)(2,1)}, u32[]{:S(2)}) %copy-start.4) | copy-done | bytes 262168
  5.4 0.0 copy-start.5
  5.4 0.9 %copy-done.5 = bf16[4,128,256]{2,1,0:T(8,128)(2,1)S(1)} copy-done((bf16[4,128,256]{2,1,0:T(8,128)(2,1)S(1)}, bf16[4,128,256]{2,1,0:T(8,128)(2,1)}, u32[]{:S(2)}) %copy-start.5) | copy-done | bytes 262168
  6.3 64.0 %two_layers.1 = (bf16[4,128,256]{2,1,0:T(8,128)(2,1)S(1)}, bf16[4,128,256]{2,1,0:T(8,128)(2,1)S(1)}) custom-call(bf16[4,128,256]{2,1,0:T(8,128)(2,1)S(1)} %copy-done, bf16[4,128,256]{2,1,0:T(8,128)(2,1)S(1)} %copy-done.1, bf16[4,128,256]{2,1,0:T(8,128)(2,1)S(1)} %copy-done.2, bf16[4,128,256]{2,1,0:T(8,128)(2,1)S(1)} %copy-done.3, ...), custom_call_target="tpu_custom_call" | custom-call | tf_op jit(solution)/shard_map/two_layers/pallas_call | solution.py:551
  70.3 0.7 copy.10
  71.0 0.7 copy.11
Async XLA Ops:
  0.6 1.0 %copy-start = (bf16[4,128,256]{2,1,0:T(8,128)(2,1)S(1)}, bf16[4,128,256]{2,1,0:T(8,128)(2,1)}, u32[]{:S(2)}) copy-start(bf16[4,128,256]{2,1,0:T(8,128)(2,1)} %qn_ref.1) | copy-start | bytes 786436
  1.6 0.9 %copy-start.1 = (bf16[4,128,256]{2,1,0:T(8,128)(2,1)S(1)}, bf16[4,128,256]{2,1,0:T(8,128)(2,1)}, u32[]{:S(2)}) copy-start(bf16[4,128,256]{2,1,0:T(8,128)(2,1)} %kn_ref.1) | copy-start | bytes 786436
  2.5 0.9 %copy-start.2 = (bf16[4,128,256]{2,1,0:T(8,128)(2,1)S(1)}, bf16[4,128,256]{2,1,0:T(8,128)(2,1)}, u32[]{:S(2)}) copy-start(bf16[4,128,256]{2,1,0:T(8,128)(2,1)} %vn_ref.1) | copy-start | bytes 786436
  3.5 0.9 %copy-start.3 = (bf16[4,128,256]{2,1,0:T(8,128)(2,1)S(1)}, bf16[4,128,256]{2,1,0:T(8,128)(2,1)}, u32[]{:S(2)}) copy-start(bf16[4,128,256]{2,1,0:T(8,128)(2,1)} %qf_ref.1) | copy-start | bytes 786436
  4.4 0.9 %copy-start.4 = (bf16[4,128,256]{2,1,0:T(8,128)(2,1)S(1)}, bf16[4,128,256]{2,1,0:T(8,128)(2,1)}, u32[]{:S(2)}) copy-start(bf16[4,128,256]{2,1,0:T(8,128)(2,1)} %kf_ref.1) | copy-start | bytes 786436
  5.4 0.9 %copy-start.5 = (bf16[4,128,256]{2,1,0:T(8,128)(2,1)S(1)}, bf16[4,128,256]{2,1,0:T(8,128)(2,1)}, u32[]{:S(2)}) copy-start(bf16[4,128,256]{2,1,0:T(8,128)(2,1)} %vf_ref.1) | copy-start | bytes 786436

commit v2 on v1

v2 whole, which is shorter than its diff:
```python
import functools
import math

import jax
import jax.numpy as jnp
from jax import lax
from jax.experimental import pallas as pl
from jax.experimental.pallas import tpu as pltpu
from jax.sharding import PartitionSpec as P

MESH = pl.DeviceIdType.MESH
HEADS = 4
HEAD = 64
CH = 256
ROWS = 4
COLS = 128
STRIP = 48
WIDE = COLS + 2 * STRIP
STEP = 16
HALF = ROWS // 2
SLOTS = 7
OWN = 3
EDGE = 16
NEAR_WIDE = COLS + 2 * EDGE
NEAR_ROWS = ROWS + 6
TILE = 32
TILES = COLS // TILE
KEYS = TILE + 2 * STRIP
NEAR_KEYS = TILE + 2 * EDGE
SCALE = math.log2(math.e) / math.sqrt(HEAD)
NONE = 99

SECOND = (
    (1, -1, -1, NONE, 1, -2, NONE, NONE),
    (NONE, NONE, 2, -1, NONE, 1, 1, -1),
    (4, 2, 2, 2, -2, -2, -2, -4),
)
FROM_STREAM = ((2, 2, 0, 0, 2, 0, 0, 0), (0, 0, 1, 2, 0, 1, 2, 2), (1, 1, 1, 1, 0, 0, 0, 0))
FROM_SECOND = ((0, 0, 1, 0, 0, 0, 0, 0), (0, 0, 0, 0, 0, 1, 0, 0), (1, 0, 0, 0, 0, 0, 0, 1))
VALUES_LAST = ((0, 5), (2, 7), ())


def pick(table, place):
    out = jnp.int32(table[0])
    for k in range(1, len(table)):
        out = jnp.where(place == k, jnp.int32(table[k]), out)
    return out


def one_of(place, places):
    out = jnp.bool_(False)
    for k in places:
        out = out | (place == k)
    return out


def kernel(
    qn_ref, kn_ref, vn_ref, qf_ref, kf_ref, vf_ref, on_ref, of_ref,
    far, near, qn, qf, qb, scores, peak, probs, total, acc, bias_far, bias_near, edge_out, edge_in, passing, out_near, out_far,
    load_sem, far_send, far_recv, strip_send, strip_recv, side_send, side_recv, extra_send, extra_recv, near_send, near_recv, pass_send, pass_recv, out_sem,
):
    row = lax.axis_index("row")
    col = lax.axis_index("col")
    n_rows = lax.axis_size("row")
    n_cols = lax.axis_size("col")
    x = row // 8
    z = (row // 4) % 2
    y = row % 4
    core = col % 2
    place = 2 * x + z
    inner = (col == 1) | (col == 2)
    true = jnp.bool_(True)

    loads = [
        pltpu.make_async_copy(kf_ref, far.at[0, OWN, :, pl.ds(STRIP, COLS)], load_sem.at[0]),
        pltpu.make_async_copy(vf_ref, far.at[1, OWN, :, pl.ds(STRIP, COLS)], load_sem.at[1]),
        pltpu.make_async_copy(kn_ref, near.at[0, pl.ds(3, ROWS), pl.ds(EDGE, COLS)], load_sem.at[2]),
        pltpu.make_async_copy(vn_ref, near.at[1, pl.ds(3, ROWS), pl.ds(EDGE, COLS)], load_sem.at[3]),
        pltpu.make_async_copy(qf_ref, qf, load_sem.at[4]),
        pltpu.make_async_copy(qn_ref, qn, load_sem.at[5]),
    ]
    for load in loads:
        load.start()

    to_row = (row + 8, row - 8, row + 4 - 8 * z)
    hop = 1 - 2 * z

    def arrivals(at, hop):
        first_ok = (at >= 2, at < 6, true)
        back = (-2, 2, hop)
        sent = [pick(SECOND[s], at + back[s]) for s in range(3)]
        second_ok = [first_ok[s] & (sent[s] != NONE) for s in range(3)]
        return (first_ok, second_ok), (back, [sent[s] + back[s] for s in range(3)])

    def slot_of(rel):
        return (rel + 10) % 7

    recv_ok, recv_rel = arrivals(place, hop)
    mate_ok, mate_rel = arrivals(place + hop, -hop)
    in_slot = [[slot_of(jnp.int32(rel)) for rel in rels] for rels in recv_rel]
    second_rel = [pick(SECOND[s], place) for s in range(3)]
    second_send = [second_rel[s] != NONE for s in range(3)]
    send_ok = ((x < 3, x > 0, true), second_send)
    shift = (-2, 2, -hop)
    src_slot = ([jnp.int32(OWN)] * 3, [slot_of(second_rel[s]) for s in range(3)])
    dst_slot = ([slot_of(jnp.int32(shift[s])) for s in range(3)], [slot_of(second_rel[s] + shift[s]) for s in range(3)])
    values_last = [one_of(place, VALUES_LAST[s]) for s in range(3)]
    late_in = [recv_ok[0][s] & one_of(place + (-2, 2, hop)[s], VALUES_LAST[s]) for s in range(3)]

    def piece(kv, hf):
        if kv == 0:
            return pl.ds(hf * HALF, HALF), pl.ds(STRIP, COLS)
        right = (col < 2) == (hf == 0)
        return pl.ds(0, ROWS), pl.ds(pl.multiple_of(jnp.where(right, STRIP + COLS // 2, STRIP), 16), COLS // 2)

    def strip_rows(kv, hf):
        return pl.ds(hf * HALF, HALF) if kv == 0 else pl.ds(0, ROWS)

    def far_copy(s, o, kv, hf):
        return pltpu.make_async_remote_copy(
            far.at[kv, src_slot[o][s], *piece(kv, hf)],
            far.at[kv, dst_slot[o][s], *piece(kv, hf)],
            far_send.at[s, o, kv, hf],
            far_recv.at[s, o, kv, hf],
            device_id=(to_row[s], col),
            device_id_type=MESH,
        )

    def send_far(s, o, kv, hf, ok=true):
        @pl.when(send_ok[o][s] & ok)
        def _():
            far_copy(s, o, kv, hf).start()

    def wait_far(s, o, kv, hf, ok=true):
        @pl.when(recv_ok[o][s] & ok)
        def _():
            block = far.at[kv, in_slot[o][s], *piece(kv, hf)]
            pltpu.make_async_remote_copy(
                block, block, far_send.at[s, o, kv, hf], far_recv.at[s, o, kv, hf],
                device_id=(to_row[s], col), device_id_type=MESH,
            ).wait_recv()

    mate = col + 1 - 2 * core
    strip_src = pl.multiple_of(jnp.where(core == 0, COLS, STRIP), 16)
    strip_dst = pl.multiple_of(jnp.where(core == 0, 0, STRIP + COLS), 16)
    strip_in = pl.multiple_of(jnp.where(core == 0, STRIP + COLS, 0), 16)

    def strip_copy(e, kv, hf, slot):
        return pltpu.make_async_remote_copy(
            far.at[kv, slot, strip_rows(kv, hf), pl.ds(strip_src, STRIP)],
            far.at[kv, slot, strip_rows(kv, hf), pl.ds(strip_dst, STRIP)],
            strip_send.at[e, kv, hf],
            strip_recv.at[e, kv, hf],
            device_id=(row, mate),
            device_id_type=MESH,
        )

    def wait_strip_at(e, kv, hf, slot):
        block = far.at[kv, slot, strip_rows(kv, hf), pl.ds(strip_in, STRIP)]
        pltpu.make_async_remote_copy(
            block, block, strip_send.at[e, kv, hf], strip_recv.at[e, kv, hf],
            device_id=(row, mate), device_id_type=MESH,
        ).wait_recv()

    def event(s, o):
        return 1 + 3 * o + s

    side_src = pl.multiple_of(jnp.where(col == 1, COLS, STRIP), 16)
    side_dst = pl.multiple_of(jnp.where(col == 1, 0, STRIP + COLS), 16)
    side_in = pl.multiple_of(jnp.where(col == 1, STRIP + COLS, 0), 16)

    def side_ok(ok, rel):
        return inner & ok & (rel >= -3) & (rel <= 3)

    def side_copy(e, kv, hf, rel):
        return pltpu.make_async_remote_copy(
            far.at[kv, slot_of(rel), strip_rows(kv, hf), pl.ds(side_src, STRIP)],
            far.at[kv, OWN + rel - hop, strip_rows(kv, hf), pl.ds(side_dst, STRIP)],
            side_send.at[e, kv, hf],
            side_recv.at[e, kv, hf],
            device_id=(to_row[2], 3 - col),
            device_id_type=MESH,
        )

    def wait_side(e, kv, hf, ok, rel):
        @pl.when(side_ok(ok, rel + hop))
        def _():
            block = far.at[kv, OWN + rel + hop, strip_rows(kv, hf), pl.ds(side_in, STRIP)]
            pltpu.make_async_remote_copy(
                block, block, side_send.at[e, kv, hf], side_recv.at[e, kv, hf],
                device_id=(to_row[2], 3 - col), device_id_type=MESH,
            ).wait_recv()

    own_rel = jnp.int32(0)
    extra_ok = (inner & (place == 4), inner & (place == 3))
    extra_slot = (0, 6)

    def extra_copy(s, kv, hf):
        return pltpu.make_async_remote_copy(
            far.at[kv, extra_slot[s], strip_rows(kv, hf), pl.ds(side_src, STRIP)],
            far.at[kv, extra_slot[s], strip_rows(kv, hf), pl.ds(side_dst, STRIP)],
            extra_send.at[kv, hf],
            extra_recv.at[kv, hf],
            device_id=(row, 3 - col),
            device_id_type=MESH,
        )

    def wait_extra(kv, hf):
        for s in range(2):
            @pl.when(extra_ok[s])
            def _():
                block = far.at[kv, extra_slot[s], strip_rows(kv, hf), pl.ds(side_in, STRIP)]
                pltpu.make_async_remote_copy(
                    block, block, extra_send.at[kv, hf], extra_recv.at[kv, hf],
                    device_id=(row, 3 - col), device_id_type=MESH,
                ).wait_recv()

    def send_strips(s, o, kv, hf, ok=true):
        ok = recv_ok[o][s] & ok
        rel = recv_rel[o][s]
        e = event(s, o)
        mine = true if kv == 0 else (inner if hf else ~inner)
        part = hf if kv == 0 else 0

        @pl.when(ok & mine)
        def _():
            strip_copy(e, kv, part, in_slot[o][s]).start()

        if kv == 0 or hf == 0:
            @pl.when(side_ok(ok, rel - hop))
            def _():
                side_copy(e, kv, part, rel).start()

            if o == 1 and s < 2:
                @pl.when(extra_ok[s] & ok)
                def _():
                    extra_copy(s, kv, part).start()

    def wait_strip(s, o, kv, hf):
        @pl.when(recv_ok[o][s])
        def _():
            wait_strip_at(event(s, o), kv, hf, in_slot[o][s])

    sides = [(dr, dc) for dr in (-1, 0, 1) for dc in (-1, 0, 1) if (dr, dc) != (0, 0)]

    def there(dr, dc):
        good = true
        if dr:
            good = good & ((row + dr >= 0) & (row + dr < n_rows))
        if dc:
            good = good & ((col + dc >= 0) & (col + dc < n_cols))
        return good

    row_src = {1: (4, 3), -1: (3, 3)}
    row_dst = {1: (0, 3), -1: (7, 3)}
    row_from = {1: 1, 0: 0, -1: 0}
    row_to = {1: 0, 0: 3, -1: 7}
    main = pl.ds(EDGE, COLS)

    def crossing(dr):
        return {0: jnp.bool_(False), 1: y == 3, -1: y == 0}[dr]

    def crossed(dr):
        return {0: jnp.bool_(False), 1: y == 0, -1: y == 3}[dr]

    def passed(dr):
        return {1: (y == 1) & (row - 2 >= 0) & (row - 2 < n_rows), -1: (y == 2) & (row + 2 >= 0) & (row + 2 < n_rows)}[dr]

    def pass_in(dr):
        return pltpu.make_async_remote_copy(
            near.at[0, pl.ds(*row_src[dr]), main],
            passing,
            pass_send.at[0],
            pass_recv.at[0],
            device_id=(row + 2 * dr, col),
            device_id_type=MESH,
        )

    def pass_on(dr):
        n = sides.index((dr, 0))
        return pltpu.make_async_remote_copy(
            passing,
            near.at[0, pl.ds(*row_dst[dr]), main],
            pass_send.at[0],
            near_recv.at[n, 0],
            device_id=(row + -1 * dr, col),
            device_id_type=MESH,
        )

    def near_copy(n, kv):
        dr, dc = sides[n]
        if dc:
            src, dst = edge_out.at[(dc + 1) // 2], edge_in.at[n]
        else:
            src, dst = near.at[kv, pl.ds(*row_src[dr]), main], near.at[kv, pl.ds(*row_dst[dr]), main]
        return pltpu.make_async_remote_copy(
            src, dst, near_send.at[n, kv], near_recv.at[n, kv], device_id=(row + dr, col + dc), device_id_type=MESH
        )

    def near_arrival(n, kv):
        dr, dc = sides[n]
        block = edge_in.at[n] if dc else near.at[kv, pl.ds(*row_dst[dr]), main]
        return pltpu.make_async_remote_copy(
            block, block, near_send.at[n, kv], near_recv.at[n, kv],
            device_id=(row - dr, col - dc), device_id_type=MESH,
        )

    barrier = pltpu.get_barrier_semaphore()
    expected = jnp.int32(0)
    for s in range(3):
        @pl.when(send_ok[0][s])
        def _():
            pl.semaphore_signal(barrier, inc=1, device_id=(to_row[s], col), device_id_type=MESH)

        expected = expected + recv_ok[0][s].astype(jnp.int32)

    @pl.when(inner)
    def _():
        pl.semaphore_signal(barrier, inc=1, device_id=(to_row[2], 3 - col), device_id_type=MESH)

    expected = expected + inner.astype(jnp.int32)
    for dr, dc in sides:
        @pl.when(there(dr, dc))
        def _():
            pl.semaphore_signal(barrier, inc=1, device_id=(row + dr, col + dc), device_id_type=MESH)

        expected = expected + there(-dr, -dc).astype(jnp.int32)
    for dr in (-1, 1):
        @pl.when(crossing(dr) & there(dr, 0))
        def _():
            pl.semaphore_signal(barrier, inc=1, device_id=(row + 2 * dr, col), device_id_type=MESH)

        @pl.when(passed(dr))
        def _():
            pl.semaphore_signal(barrier, inc=1, device_id=(row - 2 * dr, col), device_id_type=MESH)


        expected = expected + (crossing(dr) & there(dr, 0)).astype(jnp.int32) + passed(dr).astype(jnp.int32)
    pl.semaphore_wait(barrier, expected)

    for kv in range(2):
        loads[kv].wait()
        for hf in range(2):
            for s in range(3):
                send_far(s, 0, kv, hf, ok=~values_last[s] if kv else true)
            if kv == 0 or hf == 0:
                strip_copy(0, kv, hf, OWN).start()

                @pl.when(inner)
                def _():
                    side_copy(0, kv, hf, own_rel).start()

    loads[2].wait()
    loads[3].wait()
    for dc in (-1, 1):
        at = EDGE + (COLS - EDGE if dc == 1 else 0)
        inside = EDGE - 4 if dc == 1 else 0
        for kv in range(2):
            parts = [near[kv, 3 + r, at : at + EDGE, :].astype(jnp.float32)[inside : inside + 4] for r in range(ROWS)]
            edge_out[(dc + 1) // 2, kv] = jnp.concatenate(parts, axis=0).astype(jnp.bfloat16)

    def send_near(late):
        for n, (dr, dc) in enumerate(sides):
            good = there(dr, dc) & (crossing(dr) == late)
            for kv in range(1 if dc else 2):
                ok = good & ~crossing(dr) if (kv == 0 and not dc) else good

                @pl.when(ok)
                def _():
                    near_copy(n, kv).start()

        if late:
            for dr in (-1, 1):
                @pl.when(crossing(dr) & there(dr, 0))
                def _():
                    pass_in(dr).start()

    def pass_near():
        for dr in (-1, 1):
            @pl.when(passed(dr))
            def _():
                pltpu.make_async_remote_copy(
                    passing, passing, pass_send.at[0], pass_recv.at[0],
                    device_id=(row - 2 * dr, col), device_id_type=MESH,
                ).wait_recv()
                pass_on(dr).start()

    def wait_near(late):
        for n, (dr, dc) in enumerate(sides):
            @pl.when(there(-dr, -dc) & (crossing(-dr) == late))
            def _():
                near_arrival(n, 0).wait_recv()
                if dc == 0:
                    near_arrival(n, 1).wait_recv()
                else:
                    at = 0 if dc == 1 else EDGE + COLS
                    blank = jnp.zeros((EDGE - 4, CH), jnp.float32)
                    for kv in range(2):
                        packed = edge_in[n, kv].astype(jnp.float32)
                        for r in range(ROWS if dr == 0 else 3):
                            four = packed[4 * (row_from[dr] + r) : 4 * (row_from[dr] + r) + 4]
                            full = [blank, four] if dc == 1 else [four, blank]
                            near[kv, row_to[dr] + r, at : at + EDGE, :] = jnp.concatenate(full, axis=0).astype(
                                jnp.bfloat16
                            )

    send_near(False)
    send_near(True)

    c0 = col * COLS
    width = n_cols * COLS
    for t in range(TILES):
        q_at = lax.broadcasted_iota(jnp.int32, (TILE, KEYS), 0)
        k_at = lax.broadcasted_iota(jnp.int32, (TILE, KEYS), 1)
        apart = k_at - q_at
        k_col = c0 + TILE * t - STRIP + k_at
        good = ((apart & (STEP - 1)) == 0) & (apart >= 0) & (apart <= 2 * STRIP) & (k_col >= 0) & (k_col < width)
        bias_far[t] = jnp.where(good, 0.0, -jnp.inf)
    for rp in range(2):
        for t in range(TILES):
            shape = (2, TILE, 8, NEAR_KEYS)
            shape = (2 * TILE, 8 * NEAR_KEYS)
            q_id = lax.broadcasted_iota(jnp.int32, shape, 0)
            k_id = lax.broadcasted_iota(jnp.int32, shape, 1)
            r_off = (k_id // NEAR_KEYS) - (q_id // TILE)
            c_off = (k_id % NEAR_KEYS) - (q_id % TILE) - EDGE
            k_row = row * ROWS + 2 * rp - 3 + (k_id // NEAR_KEYS)
            k_col = c0 + TILE * t - EDGE + (k_id % NEAR_KEYS)
            good = (r_off >= 0) & (r_off <= 6) & (c_off >= -3) & (c_off <= 3)
            good = good & (k_row >= 0) & (k_row < n_rows * ROWS) & (k_col >= 0) & (k_col < width)
            bias_near[rp * TILES + t] = jnp.where(good, 0.0, -jnp.inf)

    zero = lambda shape: jnp.zeros(shape, jnp.bfloat16)
    for a in range(SLOTS):
        relayed = (a == 0) & (place == 0) | (a == 6) & (place == 7)
        lost = ((place + a - OWN < 0) | (place + a - OWN > 7)) & ~relayed

        @pl.when(lost)
        def _():
            for kv in range(2):
                for r in range(ROWS):
                    far[kv, a, r] = zero((WIDE, CH))

        @pl.when(~lost & (col == 0))
        def _():
            for kv in range(2):
                for r in range(ROWS):
                    far[kv, a, r, 0:STRIP] = zero((STRIP, CH))

        @pl.when(~lost & (col == 3))
        def _():
            for kv in range(2):
                for r in range(ROWS):
                    far[kv, a, r, STRIP + COLS : WIDE] = zero((STRIP, CH))

        if a in (0, 6):
            @pl.when(relayed & inner)
            def _():
                for kv in range(2):
                    for r in range(ROWS):
                        far[kv, a, r, pl.ds(side_in, STRIP)] = zero((STRIP, CH))

    for kv in range(2):
        @pl.when(row == 0)
        def _():
            near[kv, 0:3] = zero((3, NEAR_WIDE, CH))

        @pl.when(row == n_rows - 1)
        def _():
            near[kv, 7:10] = zero((3, NEAR_WIDE, CH))

        @pl.when(col == 0)
        def _():
            near[kv, :, 0:EDGE] = zero((NEAR_ROWS, EDGE, CH))

        @pl.when(col == n_cols - 1)
        def _():
            near[kv, :, EDGE + COLS : NEAR_WIDE] = zero((NEAR_ROWS, EDGE, CH))

    lane_head = lax.broadcasted_iota(jnp.int32, (1, CH), 1) // HEAD
    head_mask = [(lane_head == h).astype(jnp.float32) for h in range(HEADS)]
    head_mask_narrow = [m.astype(jnp.bfloat16) for m in head_mask]
    dims_t = (((1,), (1,)), ((), ()))
    dims = (((1,), (0,)), ((), ()))

    loads[4].wait()
    loads[5].wait()

    def block_queries(q):
        return jnp.concatenate([q * head_mask_narrow[h] for h in range(HEADS)], axis=0)

    @pl.loop(0, ROWS, unroll=2)
    def _(r):
        for t in range(TILES):
            qb[r * TILES + t] = block_queries(qf[r, TILE * t : TILE * (t + 1), :])

    half_tiles = (jnp.where(col < 2, 0, 2), jnp.where(col < 2, 2, 0))

    def score_blocks(hf, slots, part, first=False):
        row_bias = []
        for slot in slots:
            ok = (place + slot - OWN >= 0) & (place + slot - OWN <= 7)
            row_bias.append(jnp.where(ok, 0.0, -jnp.inf).astype(jnp.float32))

        @pl.loop(hf * HALF, hf * HALF + HALF, unroll=True)
        def _(r):
            for tt in range(2):
                t = half_tiles[part] + tt
                idx = r * TILES + t
                where = pl.ds(pl.multiple_of(TILE * t, TILE), KEYS)
                top = None if first else peak[idx]
                for n in range(0, len(slots), 2):
                    pair = slots[n : n + 2]
                    k = jnp.concatenate([far[0, slot, r, where, :] for slot in pair], axis=0)
                    both = lax.dot_general(qb[idx], k, dims_t, preferred_element_type=jnp.float32) * SCALE
                    for m, slot in enumerate(pair):
                        b = bias_far[t] + row_bias[n + m]
                        s = both[:, m * KEYS : (m + 1) * KEYS].reshape(HEADS, TILE, KEYS) + b[None]
                        s = s.reshape(HEADS * TILE, KEYS)
                        scores[slot, idx] = s
                        top = s if top is None else jnp.maximum(top, s)
                peak[idx] = top

    def value_sum(idx, r, t, slots, o):
        where = pl.ds(pl.multiple_of(TILE * t, TILE), KEYS)
        for n in range(0, len(slots), 2):
            pair = slots[n : n + 2]
            p = jnp.concatenate([probs[slot, idx] for slot in pair], axis=1)
            v = jnp.concatenate([far[1, slot, r, where, :] for slot in pair], axis=0)
            d = lax.dot_general(p, v, dims, preferred_element_type=jnp.float32)
            o = d if o is None else o + d
        return o

    from_stream = [pick(FROM_STREAM[s], place) for s in range(3)]
    after_first = [pick(FROM_SECOND[s], place) == 0 for s in range(3)]
    needs_second = [jnp.bool_(False)] * 3
    for s in range(3):
        for d in range(3):
            needs_second[d] = needs_second[d] | (second_send[s] & ~after_first[s] & (from_stream[s] == d))

    first_slots = (jnp.int32(1), jnp.int32(5), OWN + hop)
    second_slots = (jnp.int32(0), jnp.int32(6), OWN - hop)
    own = jnp.int32(OWN)

    def later_sides(kv, hf):
        for o in range(2):
            for s in range(3):
                if (s, o) != (2, 0):
                    wait_side(event(s, o), kv, hf, mate_ok[o][s], mate_rel[o][s])
        wait_extra(kv, hf)

    for hf in range(2):
        for s in range(3):
            wait_far(s, 0, 0, hf)
        for s in range(3):
            send_far(s, 1, 0, hf, ok=after_first[s])
        for s in range(3):
            send_strips(s, 0, 0, hf)
    for hf in range(2):
        wait_strip_at(0, 0, hf, OWN)
        for s in range(3):
            wait_strip(s, 0, 0, hf)
        score_blocks(hf, (own,) + first_slots, 0, first=True)
    for hf in range(2):
        wait_side(0, 0, hf, true, own_rel)
        wait_side(event(2, 0), 0, hf, mate_ok[0][2], mate_rel[0][2])
        score_blocks(hf, (own, first_slots[2]), 1, first=True)

    for hf in range(2):
        for s in range(3):
            wait_far(s, 0, 1, hf, ok=~late_in[s])
        for s in range(3):
            send_far(s, 1, 1, hf, ok=after_first[s])
        if hf == 1:
            for h in range(2):
                for s in range(3):
                    send_far(s, 0, 1, h, ok=values_last[s])
        for s in range(3):
            wait_far(s, 1, 0, hf, ok=needs_second[s])
        for s in range(3):
            send_far(s, 1, 0, hf, ok=~after_first[s])
        for s in range(3):
            send_strips(s, 0, 1, hf, ok=~late_in[s])

    def near_layer(rp):
        @pl.loop(0, TILES, unroll=True)
        def _(t):
            cols = pl.ds(pl.multiple_of(TILE * t, TILE), TILE)
            keys = pl.ds(pl.multiple_of(TILE * t, TILE), NEAR_KEYS)
            q = qn[pl.ds(2 * rp, 2), cols, :].reshape(2 * TILE, CH)
            k = near[0, pl.ds(2 * rp, 8), keys, :].reshape(8 * NEAR_KEYS, CH)
            v = near[1, pl.ds(2 * rp, 8), keys, :].reshape(8 * NEAR_KEYS, CH)
            s = lax.dot_general(block_queries(q), k, dims_t, preferred_element_type=jnp.float32) * SCALE
            s = s.reshape(HEADS, 2 * TILE, 8 * NEAR_KEYS) + bias_near[rp * TILES + t][None]
            s = s.reshape(HEADS * 2 * TILE, 8 * NEAR_KEYS)
            p = jnp.exp2(s - jnp.max(s, axis=1, keepdims=True))
            inverse = 1.0 / jnp.sum(p, axis=1, keepdims=True)
            o = lax.dot_general(p.astype(jnp.bfloat16), v, dims, preferred_element_type=jnp.float32) * inverse
            out = None
            for h in range(HEADS):
                part = o[h * 2 * TILE : (h + 1) * 2 * TILE] * head_mask[h]
                out = part if out is None else out + part
            out_near[pl.ds(2 * rp, 2), cols, :] = out.astype(jnp.bfloat16).reshape(2, TILE, CH)

    def relay_second_values(hf):
        for s in range(3):
            wait_far(s, 1, 1, hf, ok=needs_second[s])
        for s in range(3):
            send_far(s, 1, 1, hf, ok=~after_first[s])

    for hf in range(2):
        relay_second_values(hf)
        for s in range(3):
            wait_far(s, 1, 0, hf, ok=~needs_second[s])
        for s in range(3):
            send_strips(s, 1, 0, hf)
        if hf == 0:
            pass_near()
    for hf in range(2):
        for s in range(3):
            wait_strip(s, 1, 0, hf)
        score_blocks(hf, second_slots, 0)

    def last_values(hf):
        for s in range(2):
            wait_far(s, 0, 1, hf, ok=late_in[s])
        for s in range(2):
            send_strips(s, 0, 1, hf, ok=late_in[s])
        for s in range(3):
            wait_far(s, 1, 1, hf, ok=~needs_second[s])
        for s in range(3):
            send_strips(s, 1, 1, hf)

    later_sides(0, 0)
    later_sides(0, 1)
    last_values(0)
    for hf in range(2):
        score_blocks(hf, first_slots[:2] + second_slots, 1)

    @pl.loop(0, ROWS, unroll=2)
    def _(r):
        for t in range(TILES):
            idx = r * TILES + t
            m = jnp.max(peak[idx], axis=1, keepdims=True)
            summed = None
            for a in range(SLOTS):
                p = jnp.exp2(scores[a, idx] - m)
                probs[a, idx] = p.astype(jnp.bfloat16)
                summed = p if summed is None else summed + p
            total[idx] = jnp.broadcast_to(1.0 / jnp.sum(summed, axis=1, keepdims=True), (HEADS * TILE, 128))

    wait_strip_at(0, 1, 0, OWN)
    wait_strip(2, 0, 1, 0)
    wait_side(0, 1, 0, true, own_rel)
    wait_side(event(2, 0), 1, 0, mate_ok[0][2], mate_rel[0][2])

    @pl.loop(0, ROWS, unroll=2)
    def _(r):
        for t in range(TILES):
            idx = r * TILES + t
            acc[idx] = value_sum(idx, r, t, (own, first_slots[2]), None)

    last_values(1)
    wait_near(False)
    wait_near(True)
    near_layer(0)
    near_layer(1)
    near_out = pltpu.make_async_copy(out_near, on_ref, out_sem.at[0])
    near_out.start()
    for s in range(2):
        wait_strip(s, 0, 1, 0)
    for s in range(3):
        wait_strip(s, 1, 1, 0)
    later_sides(1, 0)

    @pl.loop(0, ROWS, unroll=2)
    def _(r):
        for t in range(TILES):
            idx = r * TILES + t
            o = value_sum(idx, r, t, first_slots[:2] + second_slots, acc[idx])
            out = None
            for h in range(HEADS):
                part = slice(h * TILE, (h + 1) * TILE)
                inverse = total[idx, part, :]
                one = o[part, :] * jnp.concatenate([inverse, inverse], axis=1) * head_mask[h]
                out = one if out is None else out + one
            out_far[r, TILE * t : TILE * (t + 1), :] = out.astype(jnp.bfloat16)

    far_out = pltpu.make_async_copy(out_far, of_ref, out_sem.at[1])
    far_out.start()

    for kv in range(2):
        for hf in range(2):
            if kv == 0 or hf == 0:
                strip_copy(0, kv, hf, OWN).wait_send()

                @pl.when(inner)
                def _():
                    side_copy(0, kv, hf, own_rel).wait_send()

                for s in range(2):
                    @pl.when(extra_ok[s])
                    def _():
                        extra_copy(s, kv, hf).wait_send()

            for o in range(2):
                for s in range(3):
                    @pl.when(send_ok[o][s])
                    def _():
                        far_copy(s, o, kv, hf).wait_send()

                    if kv == 0 or hf == 0:
                        @pl.when(recv_ok[o][s])
                        def _():
                            strip_copy(event(s, o), kv, hf, in_slot[o][s]).wait_send()

                        @pl.when(side_ok(recv_ok[o][s], recv_rel[o][s] - hop))
                        def _():
                            side_copy(event(s, o), kv, hf, recv_rel[o][s]).wait_send()

    for n, (dr, dc) in enumerate(sides):
        for kv in range(1 if dc else 2):
            good = there(dr, dc) & ~crossing(dr) if (kv == 0 and not dc) else there(dr, dc)

            @pl.when(good)
            def _():
                near_copy(n, kv).wait_send()

    for dr in (-1, 1):
        @pl.when(crossing(dr) & there(dr, 0))
        def _():
            pass_in(dr).wait_send()

        @pl.when(passed(dr))
        def _():
            pass_on(dr).wait_send()

    near_out.wait()
    far_out.wait()


def per_device(query_near, key_near, value_near, dilated_queries, dilated_keys, dilated_values):
    block = jax.ShapeDtypeStruct((ROWS, COLS, CH), jnp.bfloat16)
    tiles = ROWS * TILES
    dma = pltpu.SemaphoreType.DMA
    anywhere = pl.BlockSpec(memory_space=pl.ANY)
    return pl.pallas_call(
        kernel,
        out_shape=(block, block),
        in_specs=[pl.BlockSpec(memory_space=pltpu.HBM)] * 6,
        out_specs=(anywhere, anywhere),
        scratch_shapes=[
            pltpu.VMEM((2, SLOTS, ROWS, WIDE, CH), jnp.bfloat16),
            pltpu.VMEM((2, NEAR_ROWS, NEAR_WIDE, CH), jnp.bfloat16),
            pltpu.VMEM((ROWS, COLS, CH), jnp.bfloat16),
            pltpu.VMEM((ROWS, COLS, CH), jnp.bfloat16),
            pltpu.VMEM((tiles, HEADS * TILE, CH), jnp.bfloat16),
            pltpu.VMEM((SLOTS, tiles, HEADS * TILE, KEYS), jnp.float32),
            pltpu.VMEM((tiles, HEADS * TILE, KEYS), jnp.float32),
            pltpu.VMEM((SLOTS, tiles, HEADS * TILE, KEYS), jnp.bfloat16),
            pltpu.VMEM((tiles, HEADS * TILE, 128), jnp.float32),
            pltpu.VMEM((tiles, HEADS * TILE, CH), jnp.float32),
            pltpu.VMEM((TILES, TILE, KEYS), jnp.float32),
            pltpu.VMEM((2 * TILES, 2 * TILE, 8 * NEAR_KEYS), jnp.float32),
            pltpu.VMEM((2, 2, 4 * ROWS, CH), jnp.bfloat16),
            pltpu.VMEM((9, 2, 4 * ROWS, CH), jnp.bfloat16),
            pltpu.VMEM((3, COLS, CH), jnp.bfloat16),
            pltpu.VMEM((ROWS, COLS, CH), jnp.bfloat16),
            pltpu.VMEM((ROWS, COLS, CH), jnp.bfloat16),
            dma((6,)),
            dma((3, 2, 2, 2)),
            dma((3, 2, 2, 2)),
            dma((7, 2, 2)),
            dma((7, 2, 2)),
            dma((7, 2, 2)),
            dma((7, 2, 2)),
            dma((2, 2)),
            dma((2, 2)),
            dma((8, 2)),
            dma((8, 2)),
            dma((1,)),
            dma((1,)),
            dma((2,)),
        ],
        compiler_params=pltpu.CompilerParams(
            collective_id=0, has_side_effects=True, vmem_limit_bytes=56 << 20
        ),
        name="two_layers",
    )(query_near, key_near, value_near, dilated_queries, dilated_keys, dilated_values)


def solution(mesh):
    placed = (P("row", "col", None),) * 6
    return jax.shard_map(
        per_device,
        mesh=mesh,
        in_specs=placed,
        out_specs=(P("row", "col", None), P("row", "col", None)),
        check_vma=False,
    )
```

time: 72 us -> 52.9 us (0.73)
  the two profiles are of different devices: /device:TPU:1 before, /device:TPU:5 now
where the time goes in v2:
time: 52.9 us; the launch traced here: 52.8 us
  Pallas kernels  49.7 us (94%)
  local copies, waits for them, and re-layouts  2.42 us (5%)
  between operations  0.65 us (1%)
    pallas_call x1, Pallas kernels, per_device(): pl.pallas_call(kernel, out_shape=(block, block), in_specs=[pl.BlockSpec(m...  49.7 us
    unnamed x4, local copies, waits for them, and re-layouts  2.42 us

profile of v2, /device:TPU:5, one launch (start us, length us, event | category | flops | bytes accessed | tf_op | source)
XLA Modules:
  0.0 52.8 jit_solution(7972345274763803885)
XLA Ops:
  0.6 49.7 %two_layers.1 = (bf16[4,128,256]{2,1,0:T(8,128)(2,1)}, bf16[4,128,256]{2,1,0:T(8,128)(2,1)}) custom-call(bf16[4,128,256]{2,1,0:T(8,128)(2,1)} %qn_ref.1, bf16[4,128,256]{2,1,0:T(8,128)(2,1)} %kn_ref.1, bf16[4,128,256]{2,1,0:T(8,128)(2,1)} %vn_ref.1, bf16[4,128,256]{2,1,0:T(8,128)(2,1)} %qf_ref.1, bf16[4,128,256]{2,1,0:T(8,128)(2,1)} %kf_ref.1, ...), custom_call_target="tpu_custom_call" | custom-call | tf_op jit(solution)/shard_map/two_layers/pallas_call | solution.py:747
  50.4 0.0 copy-start
  50.4 1.7 %copy.10 = bf16[4,128,256]{2,1,0:T(8,128)(2,1)} copy(bf16[4,128,256]{2,1,0:T(8,128)(2,1)} %get-tuple-element.4) | data formatting | bytes 524288
  52.1 0.0 copy-done
  52.1 0.7 %copy.11 = bf16[4,128,256]{2,1,0:T(8,128)(2,1)} copy(bf16[4,128,256]{2,1,0:T(8,128)(2,1)S(1)} %copy-done) | data formatting | bytes 524288
Async XLA Ops:
  50.4 1.7 %copy-start = (bf16[4,128,256]{2,1,0:T(8,128)(2,1)S(1)}, bf16[4,128,256]{2,1,0:T(8,128)(2,1)}, u32[]{:S(2)}) copy-start(bf16[4,128,256]{2,1,0:T(8,128)(2,1)} %get-tuple-element.5) | copy-start | bytes 786436

commit v3 on v2

--- a/solution.py
+++ b/solution.py
@@ -192,16 +192,18 @@
             ).wait_recv()
 
     own_rel = jnp.int32(0)
-    extra_ok = (inner & (place == 4), inner & (place == 3))
-    extra_slot = (0, 6)
+    extra_ok = (inner & (place == 3), inner & (place == 4))
+    extra_from = (1, 5)
+    extra_to = (0, 6)
+    extra_row = (row + 4, row - 4)
 
     def extra_copy(s, kv, hf):
         return pltpu.make_async_remote_copy(
-            far.at[kv, extra_slot[s], strip_rows(kv, hf), pl.ds(side_src, STRIP)],
-            far.at[kv, extra_slot[s], strip_rows(kv, hf), pl.ds(side_dst, STRIP)],
+            far.at[kv, extra_from[s], strip_rows(kv, hf), pl.ds(side_src, STRIP)],
+            far.at[kv, extra_to[s], strip_rows(kv, hf), pl.ds(side_dst, STRIP)],
             extra_send.at[kv, hf],
             extra_recv.at[kv, hf],
-            device_id=(row, 3 - col),
+            device_id=(extra_row[s], 3 - col),
             device_id_type=MESH,
         )
 
@@ -209,10 +211,10 @@
         for s in range(2):
             @pl.when(extra_ok[s])
             def _():
-                block = far.at[kv, extra_slot[s], strip_rows(kv, hf), pl.ds(side_in, STRIP)]
+                block = far.at[kv, extra_to[1 - s], strip_rows(kv, hf), pl.ds(side_in, STRIP)]
                 pltpu.make_async_remote_copy(
                     block, block, extra_send.at[kv, hf], extra_recv.at[kv, hf],
-                    device_id=(row, 3 - col), device_id_type=MESH,
+                    device_id=(extra_row[s], 3 - col), device_id_type=MESH,
                 ).wait_recv()
 
     def send_strips(s, o, kv, hf, ok=true):
@@ -231,7 +233,7 @@
             def _():
                 side_copy(e, kv, part, rel).start()
 
-            if o == 1 and s < 2:
+            if o == 0 and s < 2:
                 @pl.when(extra_ok[s] & ok)
                 def _():
                     extra_copy(s, kv, part).start()
@@ -260,30 +262,35 @@
     def crossing(dr):
         return {0: jnp.bool_(False), 1: y == 3, -1: y == 0}[dr]
 
-    def crossed(dr):
-        return {0: jnp.bool_(False), 1: y == 0, -1: y == 3}[dr]
-
-    def passed(dr):
-        return {1: (y == 1) & (row - 2 >= 0) & (row - 2 < n_rows), -1: (y == 2) & (row + 2 >= 0) & (row + 2 < n_rows)}[dr]
-
-    def pass_in(dr):
+    FIRST_LEG = (2, -1)
+    LAST_LEG = (-1, 2)
+
+    def sends_pass(dr):
+        return crossing(dr) & there(dr, 0)
+
+    def passes(kv, dr):
+        at = {(0, 1): 1, (0, -1): 2, (1, 1): 2, (1, -1): 1}[kv, dr]
+        back, on = row - FIRST_LEG[kv] * dr, row + LAST_LEG[kv] * dr
+        return (y == at) & (back >= 0) & (back < n_rows) & (on >= 0) & (on < n_rows)
+
+    def pass_in(kv, dr):
         return pltpu.make_async_remote_copy(
-            near.at[0, pl.ds(*row_src[dr]), main],
-            passing,
-            pass_send.at[0],
-            pass_recv.at[0],
-            device_id=(row + 2 * dr, col),
+            near.at[kv, pl.ds(*row_src[dr]), main],
+            passing.at[kv],
+            pass_send.at[kv],
+            pass_recv.at[kv],
+            device_id=(row + FIRST_LEG[kv] * dr, col),
             device_id_type=MESH,
         )
 
-    def pass_on(dr):
+    def pass_on(kv, dr):
         n = sides.index((dr, 0))
         return pltpu.make_async_remote_copy(
-            passing,
-            near.at[0, pl.ds(*row_dst[dr]), main],
-            pass_send.at[0],
-            near_recv.at[n, 0],
-            device_id=(row + -1 * dr, col),
+            passing.at[kv],
+            near.at[kv, pl.ds(*row_dst[dr]), main],
+            pass_send.at[kv],
+            near_recv.at[n, kv],
+            device_id=(row + LAST_LEG[kv] * dr, col),
             device_id_type=MESH,
         )
 
@@ -319,6 +326,12 @@
         pl.semaphore_signal(barrier, inc=1, device_id=(to_row[2], 3 - col), device_id_type=MESH)
 
     expected = expected + inner.astype(jnp.int32)
+    for s in range(2):
+        @pl.when(extra_ok[s])
+        def _():
+            pl.semaphore_signal(barrier, inc=1, device_id=(extra_row[s], 3 - col), device_id_type=MESH)
+
+        expected = expected + extra_ok[s].astype(jnp.int32)
     for dr, dc in sides:
         @pl.when(there(dr, dc))
         def _():
@@ -326,16 +339,24 @@
 
         expected = expected + there(-dr, -dc).astype(jnp.int32)
     for dr in (-1, 1):
-        @pl.when(crossing(dr) & there(dr, 0))
+        @pl.when(sends_pass(dr))
         def _():
             pl.semaphore_signal(barrier, inc=1, device_id=(row + 2 * dr, col), device_id_type=MESH)
 
-        @pl.when(passed(dr))
+        @pl.when(passes(0, dr))
         def _():
             pl.semaphore_signal(barrier, inc=1, device_id=(row - 2 * dr, col), device_id_type=MESH)
 
-
-        expected = expected + (crossing(dr) & there(dr, 0)).astype(jnp.int32) + passed(dr).astype(jnp.int32)
+        @pl.when(passes(1, dr))
+        def _():
+            pl.semaphore_signal(barrier, inc=1, device_id=(row + 2 * dr, col), device_id_type=MESH)
+
+        @pl.when(sends_pass(-dr))
+        def _():
+            pl.semaphore_signal(barrier, inc=1, device_id=(row - 2 * dr, col), device_id_type=MESH)
+
+        for good in (sends_pass(dr), passes(0, dr), passes(1, dr), sends_pass(-dr)):
+            expected = expected + good.astype(jnp.int32)
     pl.semaphore_wait(barrier, expected)
 
     for kv in range(2):
@@ -359,35 +380,33 @@
             parts = [near[kv, 3 + r, at : at + EDGE, :].astype(jnp.float32)[inside : inside + 4] for r in range(ROWS)]
             edge_out[(dc + 1) // 2, kv] = jnp.concatenate(parts, axis=0).astype(jnp.bfloat16)
 
-    def send_near(late):
+    def send_near():
         for n, (dr, dc) in enumerate(sides):
-            good = there(dr, dc) & (crossing(dr) == late)
             for kv in range(1 if dc else 2):
-                ok = good & ~crossing(dr) if (kv == 0 and not dc) else good
-
-                @pl.when(ok)
+                @pl.when(there(dr, dc) if dc else there(dr, dc) & ~crossing(dr))
                 def _():
                     near_copy(n, kv).start()
 
-        if late:
+        for dr in (-1, 1):
+            @pl.when(sends_pass(dr))
+            def _():
+                pass_in(0, dr).start()
+                pass_in(1, dr).start()
+
+    def pass_near():
+        for kv in range(2):
             for dr in (-1, 1):
-                @pl.when(crossing(dr) & there(dr, 0))
+                @pl.when(passes(kv, dr))
                 def _():
-                    pass_in(dr).start()
-
-    def pass_near():
-        for dr in (-1, 1):
-            @pl.when(passed(dr))
-            def _():
-                pltpu.make_async_remote_copy(
-                    passing, passing, pass_send.at[0], pass_recv.at[0],
-                    device_id=(row - 2 * dr, col), device_id_type=MESH,
-                ).wait_recv()
-                pass_on(dr).start()
-
-    def wait_near(late):
+                    pltpu.make_async_remote_copy(
+                        passing.at[kv], passing.at[kv], pass_send.at[kv], pass_recv.at[kv],
+                        device_id=(row - FIRST_LEG[kv] * dr, col), device_id_type=MESH,
+                    ).wait_recv()
+                    pass_on(kv, dr).start()
+
+    def wait_near():
         for n, (dr, dc) in enumerate(sides):
-            @pl.when(there(-dr, -dc) & (crossing(-dr) == late))
+            @pl.when(there(-dr, -dc))
             def _():
                 near_arrival(n, 0).wait_recv()
                 if dc == 0:
@@ -404,8 +423,7 @@
                                 jnp.bfloat16
                             )
 
-    send_near(False)
-    send_near(True)
+    send_near()
 
     c0 = col * COLS
     width = n_cols * COLS
@@ -661,8 +679,7 @@
             acc[idx] = value_sum(idx, r, t, (own, first_slots[2]), None)
 
     last_values(1)
-    wait_near(False)
-    wait_near(True)
+    wait_near()
     near_layer(0)
     near_layer(1)
     near_out = pltpu.make_async_copy(out_near, on_ref, out_sem.at[0])
@@ -720,20 +737,19 @@
 
     for n, (dr, dc) in enumerate(sides):
         for kv in range(1 if dc else 2):
-            good = there(dr, dc) & ~crossing(dr) if (kv == 0 and not dc) else there(dr, dc)
-
-            @pl.when(good)
+            @pl.when(there(dr, dc) if dc else there(dr, dc) & ~crossing(dr))
             def _():
                 near_copy(n, kv).wait_send()
 
-    for dr in (-1, 1):
-        @pl.when(crossing(dr) & there(dr, 0))
-        def _():
-            pass_in(dr).wait_send()
-
-        @pl.when(passed(dr))
-        def _():
-            pass_on(dr).wait_send()
+    for kv in range(2):
+        for dr in (-1, 1):
+            @pl.when(sends_pass(dr))
+            def _():
+                pass_in(kv, dr).wait_send()
+
+            @pl.when(passes(kv, dr))
+            def _():
+                pass_on(kv, dr).wait_send()
 
     near_out.wait()
     far_out.wait()
@@ -764,7 +780,7 @@
             pltpu.VMEM((2 * TILES, 2 * TILE, 8 * NEAR_KEYS), jnp.float32),
             pltpu.VMEM((2, 2, 4 * ROWS, CH), jnp.bfloat16),
             pltpu.VMEM((9, 2, 4 * ROWS, CH), jnp.bfloat16),
-            pltpu.VMEM((3, COLS, CH), jnp.bfloat16),
+            pltpu.VMEM((2, 3, COLS, CH), jnp.bfloat16),
             pltpu.VMEM((ROWS, COLS, CH), jnp.bfloat16),
             pltpu.VMEM((ROWS, COLS, CH), jnp.bfloat16),
             dma((6,)),
@@ -778,8 +794,8 @@
             dma((2, 2)),
             dma((8, 2)),
             dma((8, 2)),
-            dma((1,)),
-            dma((1,)),
+            dma((2,)),
+            dma((2,)),
             dma((2,)),
         ],
         compiler_params=pltpu.CompilerParams(

time: 52.9 us -> 49.8 us (0.941)
  the two profiles are of different devices: /device:TPU:5 before, /device:TPU:1 now
where the time goes in v3:
time: 49.8 us; the launch traced here: 49.7 us
  Pallas kernels  46.6 us (94%)
  local copies, waits for them, and re-layouts  2.42 us (5%)
  between operations  0.65 us (1%)
    pallas_call x1, Pallas kernels, per_device(): pl.pallas_call(kernel, out_shape=(block, block), in_specs=[pl.BlockSpec(m...  46.6 us
    unnamed x4, local copies, waits for them, and re-layouts  2.42 us

profile of v3, /device:TPU:1, one launch (start us, length us, event | category | flops | bytes accessed | tf_op | source)
XLA Modules:
  0.0 49.7 jit_solution(17445847735087094967)
XLA Ops:
  0.6 46.6 %two_layers.1 = (bf16[4,128,256]{2,1,0:T(8,128)(2,1)}, bf16[4,128,256]{2,1,0:T(8,128)(2,1)}) custom-call(bf16[4,128,256]{2,1,0:T(8,128)(2,1)} %qn_ref.1, bf16[4,128,256]{2,1,0:T(8,128)(2,1)} %kn_ref.1, bf16[4,128,256]{2,1,0:T(8,128)(2,1)} %vn_ref.1, bf16[4,128,256]{2,1,0:T(8,128)(2,1)} %qf_ref.1, bf16[4,128,256]{2,1,0:T(8,128)(2,1)} %kf_ref.1, ...), custom_call_target="tpu_custom_call" | custom-call | tf_op jit(solution)/shard_map/two_layers/pallas_call | solution.py:763
  47.2 0.0 copy-start
  47.2 1.7 %copy.10 = bf16[4,128,256]{2,1,0:T(8,128)(2,1)} copy(bf16[4,128,256]{2,1,0:T(8,128)(2,1)} %get-tuple-element.4) | data formatting | bytes 524288
  49.0 0.0 copy-done
  49.0 0.7 %copy.11 = bf16[4,128,256]{2,1,0:T(8,128)(2,1)} copy(bf16[4,128,256]{2,1,0:T(8,128)(2,1)S(1)} %copy-done) | data formatting | bytes 524288
Async XLA Ops:
  47.2 1.7 %copy-start = (bf16[4,128,256]{2,1,0:T(8,128)(2,1)S(1)}, bf16[4,128,256]{2,1,0:T(8,128)(2,1)}, u32[]{:S(2)}) copy-start(bf16[4,128,256]{2,1,0:T(8,128)(2,1)} %get-tuple-element.5) | copy-start | bytes 786436

commit v4 on v3

--- a/solution.py
+++ b/solution.py
@@ -17,7 +17,6 @@
 STRIP = 48
 WIDE = COLS + 2 * STRIP
 STEP = 16
-HALF = ROWS // 2
 SLOTS = 7
 OWN = 3
 EDGE = 16
@@ -31,13 +30,13 @@
 NONE = 99
 
 SECOND = (
-    (1, -1, -1, NONE, 1, -2, NONE, NONE),
-    (NONE, NONE, 2, -1, NONE, 1, 1, -1),
+    (1, -1, -1, NONE, 1, NONE, -2, NONE),
+    (NONE, 2, NONE, -1, NONE, 1, 1, -1),
     (4, 2, 2, 2, -2, -2, -2, -4),
 )
-FROM_STREAM = ((2, 2, 0, 0, 2, 0, 0, 0), (0, 0, 1, 2, 0, 1, 2, 2), (1, 1, 1, 1, 0, 0, 0, 0))
+FROM_STREAM = ((2, 2, 0, 0, 2, 0, 0, 0), (0, 1, 0, 2, 0, 1, 2, 2), (0, 1, 1, 1, 0, 0, 0, 1))
 FROM_SECOND = ((0, 0, 1, 0, 0, 0, 0, 0), (0, 0, 0, 0, 0, 1, 0, 0), (1, 0, 0, 0, 0, 0, 0, 1))
-VALUES_LAST = ((0, 5), (2, 7), ())
+VALUES_LAST = ((0,), (7,), ())
 
 
 def pick(table, place):
@@ -82,15 +81,16 @@
     for load in loads:
         load.start()
 
-    to_row = (row + 8, row - 8, row + 4 - 8 * z)
+    to_row = ((row + 8) % n_rows, (row + n_rows - 8) % n_rows, row + 4 - 8 * z)
     hop = 1 - 2 * z
 
     def arrivals(at, hop):
         first_ok = (at >= 2, at < 6, true)
         back = (-2, 2, hop)
-        sent = [pick(SECOND[s], at + back[s]) for s in range(3)]
-        second_ok = [first_ok[s] & (sent[s] != NONE) for s in range(3)]
-        return (first_ok, second_ok), (back, [sent[s] + back[s] for s in range(3)])
+        sent = [pick(SECOND[s], (at + back[s] + 8) % 8) for s in range(3)]
+        second_ok = [sent[s] != NONE for s in range(3)]
+        ring = (jnp.where(at < 2, 8, 0), jnp.where(at >= 6, -8, 0), 0)
+        return (first_ok, second_ok), (back, [sent[s] + back[s] + ring[s] for s in range(3)])
 
     def slot_of(rel):
         return (rel + 10) % 7
@@ -102,24 +102,20 @@
     second_send = [second_rel[s] != NONE for s in range(3)]
     send_ok = ((x < 3, x > 0, true), second_send)
     shift = (-2, 2, -hop)
+    ring = (jnp.where(place >= 6, 8, 0), jnp.where(place < 2, -8, 0), 0)
     src_slot = ([jnp.int32(OWN)] * 3, [slot_of(second_rel[s]) for s in range(3)])
-    dst_slot = ([slot_of(jnp.int32(shift[s])) for s in range(3)], [slot_of(second_rel[s] + shift[s]) for s in range(3)])
+    dst_slot = ([slot_of(jnp.int32(shift[s])) for s in range(3)], [slot_of(second_rel[s] + shift[s] + ring[s]) for s in range(3)])
     values_last = [one_of(place, VALUES_LAST[s]) for s in range(3)]
     late_in = [recv_ok[0][s] & one_of(place + (-2, 2, hop)[s], VALUES_LAST[s]) for s in range(3)]
 
-    def piece(kv, hf):
-        if kv == 0:
-            return pl.ds(hf * HALF, HALF), pl.ds(STRIP, COLS)
-        right = (col < 2) == (hf == 0)
-        return pl.ds(0, ROWS), pl.ds(pl.multiple_of(jnp.where(right, STRIP + COLS // 2, STRIP), 16), COLS // 2)
-
-    def strip_rows(kv, hf):
-        return pl.ds(hf * HALF, HALF) if kv == 0 else pl.ds(0, ROWS)
+    def piece(hf):
+        offset = jnp.where(col < 2, (COLS, STRIP)[hf], (STRIP, 2 * STRIP)[hf])
+        return pl.ds(0, ROWS), pl.ds(pl.multiple_of(offset, 16), (STRIP, COLS - STRIP)[hf])
 
     def far_copy(s, o, kv, hf):
         return pltpu.make_async_remote_copy(
-            far.at[kv, src_slot[o][s], *piece(kv, hf)],
-            far.at[kv, dst_slot[o][s], *piece(kv, hf)],
+            far.at[kv, src_slot[o][s], *piece(hf)],
+            far.at[kv, dst_slot[o][s], *piece(hf)],
             far_send.at[s, o, kv, hf],
             far_recv.at[s, o, kv, hf],
             device_id=(to_row[s], col),
@@ -134,7 +130,7 @@
     def wait_far(s, o, kv, hf, ok=true):
         @pl.when(recv_ok[o][s] & ok)
         def _():
-            block = far.at[kv, in_slot[o][s], *piece(kv, hf)]
+            block = far.at[kv, in_slot[o][s], *piece(hf)]
             pltpu.make_async_remote_copy(
                 block, block, far_send.at[s, o, kv, hf], far_recv.at[s, o, kv, hf],
                 device_id=(to_row[s], col), device_id_type=MESH,
@@ -145,20 +141,20 @@
     strip_dst = pl.multiple_of(jnp.where(core == 0, 0, STRIP + COLS), 16)
     strip_in = pl.multiple_of(jnp.where(core == 0, STRIP + COLS, 0), 16)
 
-    def strip_copy(e, kv, hf, slot):
+    def strip_copy(e, kv, slot):
         return pltpu.make_async_remote_copy(
-            far.at[kv, slot, strip_rows(kv, hf), pl.ds(strip_src, STRIP)],
-            far.at[kv, slot, strip_rows(kv, hf), pl.ds(strip_dst, STRIP)],
-            strip_send.at[e, kv, hf],
-            strip_recv.at[e, kv, hf],
+            far.at[kv, slot, :, pl.ds(strip_src, STRIP)],
+            far.at[kv, slot, :, pl.ds(strip_dst, STRIP)],
+            strip_send.at[e, kv],
+            strip_recv.at[e, kv],
             device_id=(row, mate),
             device_id_type=MESH,
         )
 
-    def wait_strip_at(e, kv, hf, slot):
-        block = far.at[kv, slot, strip_rows(kv, hf), pl.ds(strip_in, STRIP)]
+    def wait_strip_at(e, kv, slot):
+        block = far.at[kv, slot, :, pl.ds(strip_in, STRIP)]
         pltpu.make_async_remote_copy(
-            block, block, strip_send.at[e, kv, hf], strip_recv.at[e, kv, hf],
+            block, block, strip_send.at[e, kv], strip_recv.at[e, kv],
             device_id=(row, mate), device_id_type=MESH,
         ).wait_recv()
 
@@ -172,22 +168,22 @@
     def side_ok(ok, rel):
         return inner & ok & (rel >= -3) & (rel <= 3)
 
-    def side_copy(e, kv, hf, rel):
+    def side_copy(e, kv, rel):
         return pltpu.make_async_remote_copy(
-            far.at[kv, slot_of(rel), strip_rows(kv, hf), pl.ds(side_src, STRIP)],
-            far.at[kv, OWN + rel - hop, strip_rows(kv, hf), pl.ds(side_dst, STRIP)],
-            side_send.at[e, kv, hf],
-            side_recv.at[e, kv, hf],
+            far.at[kv, slot_of(rel), :, pl.ds(side_src, STRIP)],
+            far.at[kv, OWN + rel - hop, :, pl.ds(side_dst, STRIP)],
+            side_send.at[e, kv],
+            side_recv.at[e, kv],
             device_id=(to_row[2], 3 - col),
             device_id_type=MESH,
         )
 
-    def wait_side(e, kv, hf, ok, rel):
+    def wait_side(e, kv, ok, rel):
         @pl.when(side_ok(ok, rel + hop))
         def _():
-            block = far.at[kv, OWN + rel + hop, strip_rows(kv, hf), pl.ds(side_in, STRIP)]
+            block = far.at[kv, OWN + rel + hop, :, pl.ds(side_in, STRIP)]
             pltpu.make_async_remote_copy(
-                block, block, side_send.at[e, kv, hf], side_recv.at[e, kv, hf],
+                block, block, side_send.at[e, kv], side_recv.at[e, kv],
                 device_id=(to_row[2], 3 - col), device_id_type=MESH,
             ).wait_recv()
 
@@ -197,23 +193,23 @@
     extra_to = (0, 6)
     extra_row = (row + 4, row - 4)
 
-    def extra_copy(s, kv, hf):
+    def extra_copy(s, kv):
         return pltpu.make_async_remote_copy(
-            far.at[kv, extra_from[s], strip_rows(kv, hf), pl.ds(side_src, STRIP)],
-            far.at[kv, extra_to[s], strip_rows(kv, hf), pl.ds(side_dst, STRIP)],
-            extra_send.at[kv, hf],
-            extra_recv.at[kv, hf],
+            far.at[kv, extra_from[s], :, pl.ds(side_src, STRIP)],
+            far.at[kv, extra_to[s], :, pl.ds(side_dst, STRIP)],
+            extra_send.at[kv],
+            extra_recv.at[kv],
             device_id=(extra_row[s], 3 - col),
             device_id_type=MESH,
         )
 
-    def wait_extra(kv, hf):
+    def wait_extra(kv):
         for s in range(2):
             @pl.when(extra_ok[s])
             def _():
-                block = far.at[kv, extra_to[1 - s], strip_rows(kv, hf), pl.ds(side_in, STRIP)]
+                block = far.at[kv, extra_to[1 - s], :, pl.ds(side_in, STRIP)]
                 pltpu.make_async_remote_copy(
-                    block, block, extra_send.at[kv, hf], extra_recv.at[kv, hf],
+                    block, block, extra_send.at[kv], extra_recv.at[kv],
                     device_id=(extra_row[s], 3 - col), device_id_type=MESH,
                 ).wait_recv()
 
@@ -221,27 +217,25 @@
         ok = recv_ok[o][s] & ok
         rel = recv_rel[o][s]
         e = event(s, o)
-        mine = true if kv == 0 else (inner if hf else ~inner)
-        part = hf if kv == 0 else 0
-
-        @pl.when(ok & mine)
-        def _():
-            strip_copy(e, kv, part, in_slot[o][s]).start()
-
-        if kv == 0 or hf == 0:
+
+        @pl.when(ok & (inner if hf else ~inner))
+        def _():
+            strip_copy(e, kv, in_slot[o][s]).start()
+
+        if hf == 0:
             @pl.when(side_ok(ok, rel - hop))
             def _():
-                side_copy(e, kv, part, rel).start()
+                side_copy(e, kv, rel).start()
 
             if o == 0 and s < 2:
                 @pl.when(extra_ok[s] & ok)
                 def _():
-                    extra_copy(s, kv, part).start()
-
-    def wait_strip(s, o, kv, hf):
+                    extra_copy(s, kv).start()
+
+    def wait_strip(s, o, kv):
         @pl.when(recv_ok[o][s])
         def _():
-            wait_strip_at(event(s, o), kv, hf, in_slot[o][s])
+            wait_strip_at(event(s, o), kv, in_slot[o][s])
 
     sides = [(dr, dc) for dr in (-1, 0, 1) for dc in (-1, 0, 1) if (dr, dc) != (0, 0)]
 
@@ -321,6 +315,13 @@
 
         expected = expected + recv_ok[0][s].astype(jnp.int32)
 
+    for s, places in ((0, (6, 7)), (1, (0, 1))):
+        @pl.when(one_of(place, places))
+        def _():
+            pl.semaphore_signal(barrier, inc=1, device_id=(to_row[s], col), device_id_type=MESH)
+
+        expected = expected + one_of(place, places).astype(jnp.int32)
+
     @pl.when(inner)
     def _():
         pl.semaphore_signal(barrier, inc=1, device_id=(to_row[2], 3 - col), device_id_type=MESH)
@@ -359,17 +360,18 @@
             expected = expected + good.astype(jnp.int32)
     pl.semaphore_wait(barrier, expected)
 
-    for kv in range(2):
-        loads[kv].wait()
-        for hf in range(2):
+    for hf in range(2):
+        for kv in range(2):
+            if hf == 0:
+                loads[kv].wait()
             for s in range(3):
-                send_far(s, 0, kv, hf, ok=~values_last[s] if kv else true)
-            if kv == 0 or hf == 0:
-                strip_copy(0, kv, hf, OWN).start()
+                send_far(s, 0, kv, hf, ok=~values_last[s] if (kv and hf) else true)
+            if hf == 0:
+                strip_copy(0, kv, OWN).start()
 
                 @pl.when(inner)
                 def _():
-                    side_copy(0, kv, hf, own_rel).start()
+                    side_copy(0, kv, own_rel).start()
 
     loads[2].wait()
     loads[3].wait()
@@ -514,13 +516,13 @@
 
     half_tiles = (jnp.where(col < 2, 0, 2), jnp.where(col < 2, 2, 0))
 
-    def score_blocks(hf, slots, part, first=False):
+    def score_blocks(slots, part, first=False):
         row_bias = []
         for slot in slots:
             ok = (place + slot - OWN >= 0) & (place + slot - OWN <= 7)
             row_bias.append(jnp.where(ok, 0.0, -jnp.inf).astype(jnp.float32))
 
-        @pl.loop(hf * HALF, hf * HALF + HALF, unroll=True)
+        @pl.loop(0, ROWS, unroll=2)
         def _(r):
             for tt in range(2):
                 t = half_tiles[part] + tt
@@ -560,45 +562,54 @@
     second_slots = (jnp.int32(0), jnp.int32(6), OWN - hop)
     own = jnp.int32(OWN)
 
-    def later_sides(kv, hf):
+    def later_sides(kv):
         for o in range(2):
             for s in range(3):
                 if (s, o) != (2, 0):
-                    wait_side(event(s, o), kv, hf, mate_ok[o][s], mate_rel[o][s])
-        wait_extra(kv, hf)
-
-    for hf in range(2):
+                    wait_side(event(s, o), kv, mate_ok[o][s], mate_rel[o][s])
+        wait_extra(kv)
+
+    def first_arrivals(kv, hf):
+        late = kv == 1 and hf == 1
         for s in range(3):
-            wait_far(s, 0, 0, hf)
+            wait_far(s, 0, kv, hf, ok=~late_in[s] if late else true)
         for s in range(3):
-            send_far(s, 1, 0, hf, ok=after_first[s])
+            send_far(s, 1, kv, hf, ok=after_first[s])
+        if late:
+            for s in range(3):
+                send_far(s, 0, kv, hf, ok=values_last[s])
         for s in range(3):
-            send_strips(s, 0, 0, hf)
-    for hf in range(2):
-        wait_strip_at(0, 0, hf, OWN)
+            send_strips(s, 0, kv, hf, ok=~late_in[s] if late else true)
+
+    def second_that_go_on(kv, hf):
         for s in range(3):
-            wait_strip(s, 0, 0, hf)
-        score_blocks(hf, (own,) + first_slots, 0, first=True)
-    for hf in range(2):
-        wait_side(0, 0, hf, true, own_rel)
-        wait_side(event(2, 0), 0, hf, mate_ok[0][2], mate_rel[0][2])
-        score_blocks(hf, (own, first_slots[2]), 1, first=True)
-
-    for hf in range(2):
+            wait_far(s, 1, kv, hf, ok=needs_second[s])
         for s in range(3):
-            wait_far(s, 0, 1, hf, ok=~late_in[s])
+            send_far(s, 1, kv, hf, ok=~after_first[s])
+
+    def second_arrivals(kv, hf):
         for s in range(3):
-            send_far(s, 1, 1, hf, ok=after_first[s])
-        if hf == 1:
-            for h in range(2):
-                for s in range(3):
-                    send_far(s, 0, 1, h, ok=values_last[s])
+            wait_far(s, 1, kv, hf, ok=~needs_second[s])
         for s in range(3):
-            wait_far(s, 1, 0, hf, ok=needs_second[s])
-        for s in range(3):
-            send_far(s, 1, 0, hf, ok=~after_first[s])
-        for s in range(3):
-            send_strips(s, 0, 1, hf, ok=~late_in[s])
+            send_strips(s, 1, kv, hf)
+
+    first_arrivals(0, 0)
+    first_arrivals(1, 0)
+    first_arrivals(0, 1)
+    wait_strip_at(0, 0, OWN)
+    for s in range(3):
+        wait_strip(s, 0, 0)
+    score_blocks((own,) + first_slots, 0, first=True)
+    wait_side(0, 0, true, own_rel)
+    wait_side(event(2, 0), 0, mate_ok[0][2], mate_rel[0][2])
+    score_blocks((own, first_slots[2]), 1, first=True)
+    second_that_go_on(0, 0)
+    first_arrivals(1, 1)
+    second_that_go_on(1, 0)
+    second_arrivals(0, 0)
+    pass_near()
+    second_that_go_on(0, 1)
+    second_arrivals(1, 0)
 
     def near_layer(rp):
         @pl.loop(0, TILES, unroll=True)
@@ -620,40 +631,13 @@
                 out = part if out is None else out + part
             out_near[pl.ds(2 * rp, 2), cols, :] = out.astype(jnp.bfloat16).reshape(2, TILE, CH)
 
-    def relay_second_values(hf):
-        for s in range(3):
-            wait_far(s, 1, 1, hf, ok=needs_second[s])
-        for s in range(3):
-            send_far(s, 1, 1, hf, ok=~after_first[s])
-
-    for hf in range(2):
-        relay_second_values(hf)
-        for s in range(3):
-            wait_far(s, 1, 0, hf, ok=~needs_second[s])
-        for s in range(3):
-            send_strips(s, 1, 0, hf)
-        if hf == 0:
-            pass_near()
-    for hf in range(2):
-        for s in range(3):
-            wait_strip(s, 1, 0, hf)
-        score_blocks(hf, second_slots, 0)
-
-    def last_values(hf):
-        for s in range(2):
-            wait_far(s, 0, 1, hf, ok=late_in[s])
-        for s in range(2):
-            send_strips(s, 0, 1, hf, ok=late_in[s])
-        for s in range(3):
-            wait_far(s, 1, 1, hf, ok=~needs_second[s])
-        for s in range(3):
-            send_strips(s, 1, 1, hf)
-
-    later_sides(0, 0)
-    later_sides(0, 1)
-    last_values(0)
-    for hf in range(2):
-        score_blocks(hf, first_slots[:2] + second_slots, 1)
+    second_arrivals(0, 1)
+    second_that_go_on(1, 1)
+    for s in range(3):
+        wait_strip(s, 1, 0)
+    score_blocks(second_slots, 0)
+    later_sides(0)
+    score_blocks(first_slots[:2] + second_slots, 1)
 
     @pl.loop(0, ROWS, unroll=2)
     def _(r):
@@ -667,10 +651,10 @@
                 summed = p if summed is None else summed + p
             total[idx] = jnp.broadcast_to(1.0 / jnp.sum(summed, axis=1, keepdims=True), (HEADS * TILE, 128))
 
-    wait_strip_at(0, 1, 0, OWN)
-    wait_strip(2, 0, 1, 0)
-    wait_side(0, 1, 0, true, own_rel)
-    wait_side(event(2, 0), 1, 0, mate_ok[0][2], mate_rel[0][2])
+    wait_strip_at(0, 1, OWN)
+    wait_strip(2, 0, 1)
+    wait_side(0, 1, true, own_rel)
+    wait_side(event(2, 0), 1, mate_ok[0][2], mate_rel[0][2])
 
     @pl.loop(0, ROWS, unroll=2)
     def _(r):
@@ -678,17 +662,21 @@
             idx = r * TILES + t
             acc[idx] = value_sum(idx, r, t, (own, first_slots[2]), None)
 
-    last_values(1)
+    for s in range(2):
+        wait_far(s, 0, 1, 1, ok=late_in[s])
+    for s in range(2):
+        send_strips(s, 0, 1, 1, ok=late_in[s])
+    second_arrivals(1, 1)
     wait_near()
     near_layer(0)
     near_layer(1)
     near_out = pltpu.make_async_copy(out_near, on_ref, out_sem.at[0])
     near_out.start()
     for s in range(2):
-        wait_strip(s, 0, 1, 0)
+        wait_strip(s, 0, 1)
     for s in range(3):
-        wait_strip(s, 1, 1, 0)
-    later_sides(1, 0)
+        wait_strip(s, 1, 1)
+    later_sides(1)
 
     @pl.loop(0, ROWS, unroll=2)
     def _(r):
@@ -707,33 +695,31 @@
     far_out.start()
 
     for kv in range(2):
-        for hf in range(2):
-            if kv == 0 or hf == 0:
-                strip_copy(0, kv, hf, OWN).wait_send()
-
-                @pl.when(inner)
+        strip_copy(0, kv, OWN).wait_send()
+
+        @pl.when(inner)
+        def _():
+            side_copy(0, kv, own_rel).wait_send()
+
+        for s in range(2):
+            @pl.when(extra_ok[s])
+            def _():
+                extra_copy(s, kv).wait_send()
+
+        for o in range(2):
+            for s in range(3):
+                @pl.when(send_ok[o][s])
                 def _():
-                    side_copy(0, kv, hf, own_rel).wait_send()
-
-                for s in range(2):
-                    @pl.when(extra_ok[s])
-                    def _():
-                        extra_copy(s, kv, hf).wait_send()
-
-            for o in range(2):
-                for s in range(3):
-                    @pl.when(send_ok[o][s])
-                    def _():
-                        far_copy(s, o, kv, hf).wait_send()
-
-                    if kv == 0 or hf == 0:
-                        @pl.when(recv_ok[o][s])
-                        def _():
-                            strip_copy(event(s, o), kv, hf, in_slot[o][s]).wait_send()
-
-                        @pl.when(side_ok(recv_ok[o][s], recv_rel[o][s] - hop))
-                        def _():
-                            side_copy(event(s, o), kv, hf, recv_rel[o][s]).wait_send()
+                    far_copy(s, o, kv, 0).wait_send()
+                    far_copy(s, o, kv, 1).wait_send()
+
+                @pl.when(recv_ok[o][s])
+                def _():
+                    strip_copy(event(s, o), kv, in_slot[o][s]).wait_send()
+
+                @pl.when(side_ok(recv_ok[o][s], recv_rel[o][s] - hop))
+                def _():
+                    side_copy(event(s, o), kv, recv_rel[o][s]).wait_send()
 
     for n, (dr, dc) in enumerate(sides):
         for kv in range(1 if dc else 2):
@@ -755,12 +741,30 @@
     far_out.wait()
 
 
+def finish_kernel(near_ref, far_ref, near_out_ref, far_out_ref, near_held, far_held, sem):
+    first = [
+        pltpu.make_async_copy(near_ref, near_held, sem.at[0]),
+        pltpu.make_async_copy(far_ref, far_held, sem.at[1]),
+    ]
+    second = [
+        pltpu.make_async_copy(near_held, near_out_ref, sem.at[0]),
+        pltpu.make_async_copy(far_held, far_out_ref, sem.at[1]),
+    ]
+    for copy in first:
+        copy.start()
+    for n in range(2):
+        first[n].wait()
+        second[n].start()
+    for copy in second:
+        copy.wait()
+
+
 def per_device(query_near, key_near, value_near, dilated_queries, dilated_keys, dilated_values):
     block = jax.ShapeDtypeStruct((ROWS, COLS, CH), jnp.bfloat16)
     tiles = ROWS * TILES
     dma = pltpu.SemaphoreType.DMA
     anywhere = pl.BlockSpec(memory_space=pl.ANY)
-    return pl.pallas_call(
+    results = pl.pallas_call(
         kernel,
         out_shape=(block, block),
         in_specs=[pl.BlockSpec(memory_space=pltpu.HBM)] * 6,
@@ -786,12 +790,12 @@
             dma((6,)),
             dma((3, 2, 2, 2)),
             dma((3, 2, 2, 2)),
-            dma((7, 2, 2)),
-            dma((7, 2, 2)),
-            dma((7, 2, 2)),
-            dma((7, 2, 2)),
-            dma((2, 2)),
-            dma((2, 2)),
+            dma((7, 2)),
+            dma((7, 2)),
+            dma((7, 2)),
+            dma((7, 2)),
+            dma((2,)),
+            dma((2,)),
             dma((8, 2)),
             dma((8, 2)),
             dma((2,)),
@@ -803,6 +807,19 @@
         ),
         name="two_layers",
     )(query_near, key_near, value_near, dilated_queries, dilated_keys, dilated_values)
+    return pl.pallas_call(
+        finish_kernel,
+        out_shape=(block, block),
+        in_specs=[anywhere] * 2,
+        out_specs=(anywhere, anywhere),
+        scratch_shapes=[
+            pltpu.VMEM((ROWS, COLS, CH), jnp.bfloat16),
+            pltpu.VMEM((ROWS, COLS, CH), jnp.bfloat16),
+            dma((2,)),
+        ],
+        compiler_params=pltpu.CompilerParams(vmem_limit_bytes=56 << 20),
+        name="results_out",
+    )(*results)
 
 
 def solution(mesh):

time: 49.8 us -> 46.4 us (0.932)
  the two profiles are of different devices: /device:TPU:1 before, /device:TPU:4 now
where the time goes in v4:
time: 46.4 us; the launch traced here: 46.2 us
  Pallas kernels  45.6 us (98%)
  between operations  0.64 us (1%)
    pallas_call x1, Pallas kernels, per_device(): pl.pallas_call(kernel, out_shape=(block, block), in_specs=[pl.BlockSpec(m...  43.9 us
    pallas_call x1, Pallas kernels, per_device(): pl.pallas_call(finish_kernel, out_shape=(block, block), in_specs=[anywher...  1.76 us

profile of v4, /device:TPU:4, one launch (start us, length us, event | category | flops | bytes accessed | tf_op | source)
XLA Modules:
  0.0 46.2 jit_solution(10307876187128726556)
XLA Ops:
  0.6 43.9 %two_layers.1 = (bf16[4,128,256]{2,1,0:T(8,128)(2,1)}, bf16[4,128,256]{2,1,0:T(8,128)(2,1)}) custom-call(bf16[4,128,256]{2,1,0:T(8,128)(2,1)} %qn_ref.1, bf16[4,128,256]{2,1,0:T(8,128)(2,1)} %kn_ref.1, bf16[4,128,256]{2,1,0:T(8,128)(2,1)} %vn_ref.1, bf16[4,128,256]{2,1,0:T(8,128)(2,1)} %qf_ref.1, bf16[4,128,256]{2,1,0:T(8,128)(2,1)} %kf_ref.1, ...), custom_call_target="tpu_custom_call" | custom-call | tf_op jit(solution)/shard_map/two_layers/pallas_call | solution.py:767
  44.5 1.8 %results_out.1 = (bf16[4,128,256]{2,1,0:T(8,128)(2,1)}, bf16[4,128,256]{2,1,0:T(8,128)(2,1)}) custom-call(bf16[4,128,256]{2,1,0:T(8,128)(2,1)} %get-tuple-element.4.near_ref, bf16[4,128,256]{2,1,0:T(8,128)(2,1)} %get-tuple-element.5.far_ref), custom_call_target="tpu_custom_call" | custom-call | tf_op jit(solution)/shard_map/results_out/pallas_call | solution.py:810

commit v5 on v4

--- a/solution.py
+++ b/solution.py
@@ -55,7 +55,7 @@
 
 def kernel(
     qn_ref, kn_ref, vn_ref, qf_ref, kf_ref, vf_ref, on_ref, of_ref,
-    far, near, qn, qf, qb, scores, peak, probs, total, acc, bias_far, bias_near, edge_out, edge_in, passing, out_near, out_far,
+    far, near, qn, qf, qb, scores, peak, top, probs, total, acc, bias_far, bias_near, edge_out, edge_in, passing, out_near, out_far,
     load_sem, far_send, far_recv, strip_send, strip_recv, side_send, side_recv, extra_send, extra_recv, near_send, near_recv, pass_send, pass_recv, out_sem,
 ):
     row = lax.axis_index("row")
@@ -438,7 +438,6 @@
         bias_far[t] = jnp.where(good, 0.0, -jnp.inf)
     for rp in range(2):
         for t in range(TILES):
-            shape = (2, TILE, 8, NEAR_KEYS)
             shape = (2 * TILE, 8 * NEAR_KEYS)
             q_id = lax.broadcasted_iota(jnp.int32, shape, 0)
             k_id = lax.broadcasted_iota(jnp.int32, shape, 1)
@@ -631,13 +630,11 @@
                 out = part if out is None else out + part
             out_near[pl.ds(2 * rp, 2), cols, :] = out.astype(jnp.bfloat16).reshape(2, TILE, CH)
 
-    second_arrivals(0, 1)
-    second_that_go_on(1, 1)
-    for s in range(3):
-        wait_strip(s, 1, 0)
-    score_blocks(second_slots, 0)
     later_sides(0)
-    score_blocks(first_slots[:2] + second_slots, 1)
+    score_blocks(first_slots[:2], 1)
+
+    def spread(column):
+        return jnp.broadcast_to(column, (HEADS * TILE, KEYS))
 
     @pl.loop(0, ROWS, unroll=2)
     def _(r):
@@ -645,11 +642,12 @@
             idx = r * TILES + t
             m = jnp.max(peak[idx], axis=1, keepdims=True)
             summed = None
-            for a in range(SLOTS):
-                p = jnp.exp2(scores[a, idx] - m)
-                probs[a, idx] = p.astype(jnp.bfloat16)
+            for slot in (own,) + first_slots:
+                p = jnp.exp2(scores[slot, idx] - m)
+                probs[slot, idx] = p.astype(jnp.bfloat16)
                 summed = p if summed is None else summed + p
-            total[idx] = jnp.broadcast_to(1.0 / jnp.sum(summed, axis=1, keepdims=True), (HEADS * TILE, 128))
+            top[idx] = spread(m)
+            total[idx] = spread(jnp.sum(summed, axis=1, keepdims=True))
 
     wait_strip_at(0, 1, OWN)
     wait_strip(2, 0, 1)
@@ -661,6 +659,27 @@
         for t in range(TILES):
             idx = r * TILES + t
             acc[idx] = value_sum(idx, r, t, (own, first_slots[2]), None)
+
+    second_arrivals(0, 1)
+    second_that_go_on(1, 1)
+    for s in range(3):
+        wait_strip(s, 1, 0)
+    score_blocks(second_slots, 0, first=True)
+    score_blocks(second_slots, 1, first=True)
+
+    @pl.loop(0, ROWS, unroll=2)
+    def _(r):
+        for t in range(TILES):
+            idx = r * TILES + t
+            m = jnp.maximum(top[idx], spread(jnp.max(peak[idx], axis=1, keepdims=True)))
+            summed = None
+            for slot in second_slots:
+                p = jnp.exp2(scores[slot, idx] - m)
+                probs[slot, idx] = p.astype(jnp.bfloat16)
+                summed = p if summed is None else summed + p
+            scale = jnp.exp2(top[idx] - m)
+            top[idx] = scale
+            total[idx] = 1.0 / (total[idx] * scale + spread(jnp.sum(summed, axis=1, keepdims=True)))
 
     for s in range(2):
         wait_far(s, 0, 1, 1, ok=late_in[s])
@@ -682,7 +701,9 @@
     def _(r):
         for t in range(TILES):
             idx = r * TILES + t
-            o = value_sum(idx, r, t, first_slots[:2] + second_slots, acc[idx])
+            scale = top[idx]
+            o = value_sum(idx, r, t, first_slots[:2], acc[idx]) * jnp.concatenate([scale, scale], axis=1)
+            o = value_sum(idx, r, t, second_slots, o)
             out = None
             for h in range(HEADS):
                 part = slice(h * TILE, (h + 1) * TILE)
@@ -776,6 +797,7 @@
             pltpu.VMEM((ROWS, COLS, CH), jnp.bfloat16),
             pltpu.VMEM((tiles, HEADS * TILE, CH), jnp.bfloat16),
             pltpu.VMEM((SLOTS, tiles, HEADS * TILE, KEYS), jnp.float32),
+            pltpu.VMEM((tiles, HEADS * TILE, KEYS), jnp.float32),
             pltpu.VMEM((tiles, HEADS * TILE, KEYS), jnp.float32),
             pltpu.VMEM((SLOTS, tiles, HEADS * TILE, KEYS), jnp.bfloat16),
             pltpu.VMEM((tiles, HEADS * TILE, 128), jnp.float32),

time: 46.4 us -> 45.8 us (0.987)
  the two profiles are of different devices: /device:TPU:4 before, /device:TPU:35 now
where the time goes in v5:
time: 45.8 us; the launch traced here: 45.7 us
  Pallas kernels  45 us (98%)
  between operations  0.64 us (1%)
    pallas_call x1, Pallas kernels, per_device(): pl.pallas_call(kernel, out_shape=(block, block), in_specs=[pl.BlockSpec(m...  43.3 us
    pallas_call x1, Pallas kernels, per_device(): pl.pallas_call(finish_kernel, out_shape=(block, block), in_specs=[anywher...  1.76 us

profile of v5, /device:TPU:35, one launch (start us, length us, event | category | flops | bytes accessed | tf_op | source)
XLA Modules:
  0.0 45.7 jit_solution(8557495250793671508)
XLA Ops:
  0.6 43.3 %two_layers.1 = (bf16[4,128,256]{2,1,0:T(8,128)(2,1)}, bf16[4,128,256]{2,1,0:T(8,128)(2,1)}) custom-call(bf16[4,128,256]{2,1,0:T(8,128)(2,1)} %qn_ref.1, bf16[4,128,256]{2,1,0:T(8,128)(2,1)} %kn_ref.1, bf16[4,128,256]{2,1,0:T(8,128)(2,1)} %vn_ref.1, bf16[4,128,256]{2,1,0:T(8,128)(2,1)} %qf_ref.1, bf16[4,128,256]{2,1,0:T(8,128)(2,1)} %kf_ref.1, ...), custom_call_target="tpu_custom_call" | custom-call | tf_op jit(solution)/shard_map/two_layers/pallas_call | solution.py:788
  43.9 1.8 %results_out.1 = (bf16[4,128,256]{2,1,0:T(8,128)(2,1)}, bf16[4,128,256]{2,1,0:T(8,128)(2,1)}) custom-call(bf16[4,128,256]{2,1,0:T(8,128)(2,1)} %get-tuple-element.4.near_ref, bf16[4,128,256]{2,1,0:T(8,128)(2,1)} %get-tuple-element.5.far_ref), custom_call_target="tpu_custom_call" | custom-call | tf_op jit(solution)/shard_map/results_out/pallas_call | solution.py:832

commit v6 on v5

--- a/solution.py
+++ b/solution.py
@@ -508,7 +508,7 @@
     def block_queries(q):
         return jnp.concatenate([q * head_mask_narrow[h] for h in range(HEADS)], axis=0)
 
-    @pl.loop(0, ROWS, unroll=2)
+    @pl.loop(0, ROWS, unroll=True)
     def _(r):
         for t in range(TILES):
             qb[r * TILES + t] = block_queries(qf[r, TILE * t : TILE * (t + 1), :])
@@ -521,7 +521,7 @@
             ok = (place + slot - OWN >= 0) & (place + slot - OWN <= 7)
             row_bias.append(jnp.where(ok, 0.0, -jnp.inf).astype(jnp.float32))
 
-        @pl.loop(0, ROWS, unroll=2)
+        @pl.loop(0, ROWS, unroll=True)
         def _(r):
             for tt in range(2):
                 t = half_tiles[part] + tt
@@ -636,7 +636,7 @@
     def spread(column):
         return jnp.broadcast_to(column, (HEADS * TILE, KEYS))
 
-    @pl.loop(0, ROWS, unroll=2)
+    @pl.loop(0, ROWS, unroll=True)
     def _(r):
         for t in range(TILES):
             idx = r * TILES + t
@@ -654,7 +654,7 @@
     wait_side(0, 1, true, own_rel)
     wait_side(event(2, 0), 1, mate_ok[0][2], mate_rel[0][2])
 
-    @pl.loop(0, ROWS, unroll=2)
+    @pl.loop(0, ROWS, unroll=True)
     def _(r):
         for t in range(TILES):
             idx = r * TILES + t
@@ -667,7 +667,7 @@
     score_blocks(second_slots, 0, first=True)
     score_blocks(second_slots, 1, first=True)
 
-    @pl.loop(0, ROWS, unroll=2)
+    @pl.loop(0, ROWS, unroll=True)
     def _(r):
         for t in range(TILES):
             idx = r * TILES + t
@@ -697,7 +697,7 @@
         wait_strip(s, 1, 1)
     later_sides(1)
 
-    @pl.loop(0, ROWS, unroll=2)
+    @pl.loop(0, ROWS, unroll=True)
     def _(r):
         for t in range(TILES):
             idx = r * TILES + t

time: 45.8 us -> 44.8 us (0.978)
  Pallas kernels: 45 us -> 44 us
    pallas_call x1, Pallas kernels: 43.3 us -> 42.3 us  [per_device(): pl.pallas_call(kernel, out_shape=(block, block), in_specs=[pl.BlockSpec(m...]
where the time goes in v6:
time: 44.8 us; the launch traced here: 44.7 us
  Pallas kernels  44 us (98%)
  between operations  0.64 us (1%)
    pallas_call x1, Pallas kernels, per_device(): pl.pallas_call(kernel, out_shape=(block, block), in_specs=[pl.BlockSpec(m...  42.3 us
    pallas_call x1, Pallas kernels, per_device(): pl.pallas_call(finish_kernel, out_shape=(block, block), in_specs=[anywher...  1.76 us

profile of v6, /device:TPU:35, one launch (start us, length us, event | category | flops | bytes accessed | tf_op | source)
XLA Modules:
  0.0 44.7 jit_solution(4252974334651516808)
XLA Ops:
  0.6 42.3 %two_layers.1 = (bf16[4,128,256]{2,1,0:T(8,128)(2,1)}, bf16[4,128,256]{2,1,0:T(8,128)(2,1)}) custom-call(bf16[4,128,256]{2,1,0:T(8,128)(2,1)} %qn_ref.1, bf16[4,128,256]{2,1,0:T(8,128)(2,1)} %kn_ref.1, bf16[4,128,256]{2,1,0:T(8,128)(2,1)} %vn_ref.1, bf16[4,128,256]{2,1,0:T(8,128)(2,1)} %qf_ref.1, bf16[4,128,256]{2,1,0:T(8,128)(2,1)} %kf_ref.1, ...), custom_call_target="tpu_custom_call" | custom-call | tf_op jit(solution)/shard_map/two_layers/pallas_call | solution.py:788
  42.9 1.8 %results_out.1 = (bf16[4,128,256]{2,1,0:T(8,128)(2,1)}, bf16[4,128,256]{2,1,0:T(8,128)(2,1)}) custom-call(bf16[4,128,256]{2,1,0:T(8,128)(2,1)} %get-tuple-element.4.near_ref, bf16[4,128,256]{2,1,0:T(8,128)(2,1)} %get-tuple-element.5.far_ref), custom_call_target="tpu_custom_call" | custom-call | tf_op jit(solution)/shard_map/results_out/pallas_call | solution.py:832
